TPU v7x, 32 devices: a whole 2x2x4 slice. The times are simulated.
32 devices in a mesh: lon: 8 (over y, x, core), lat: 4 (over z).
Axes of the slice: x: 2, y: 2, z: 4, core: 2. Of those that a mesh axis runs over, the one named last changes fastest.
Arguments:
- velocity: float32 [2, 4, 256, 4096], P(None, None, 'lat', 'lon'), may hold values from -3 to 3
- thickness: float32 [4, 256, 4096], P(None, 'lat', 'lon'), may hold values from -6 to 6
- tracers: float32 [2, 4, 256, 4096], P(None, None, 'lat', 'lon'), may hold values from -6 to 6
- land_mask: int32 [4, 256, 4096], P(None, 'lat', 'lon'), may hold values from 0 to 1, as said below
Outputs:
- velocity_out: float32 [2, 4, 256, 4096], P(None, None, 'lat', 'lon')
- thickness_out: float32 [4, 256, 4096], P(None, 'lat', 'lon')
- tracers_out: float32 [2, 4, 256, 4096], P(None, None, 'lat', 'lon')
Inputs may be any that keep to these rules, and one draw needn't show every extreme that they name: `land_mask`: A level is ocean only where every level above it is ocean.
All inputs are finite; a program needn't handle non-finite values.
Results may differ from a plain program's by a relative error of at most 0.00002.
Values sent between devices are 32-bit elements; how exact they have to be, the bound alone decides.
No kernel may reach another device: no remote copies, remote signals or barrier semaphores. Data moves between devices by JAX's collectives and lax.ppermute only.
A program may use at most 64 MiB of HBM per device.

v0:
```python
import functools

import jax
import jax.numpy as jnp
from jax import lax
from jax.experimental import pallas as pl
from jax.experimental.pallas import tpu as pltpu
from jax.sharding import PartitionSpec as P

ADVECTION = 0.25
DIFFUSION = 0.05
HYPERVISCOSITY = 0.02
CORIOLIS = 0.3
GRADIENT = 0.2
CONVERGENCE = 0.3

HALO = 4
PAD = 8
LANES = 128
SUB = 8
SLOTS = 11
F32 = jnp.float32
VMEM = pl.BlockSpec(memory_space=pltpu.VMEM)
HBM = pl.BlockSpec(memory_space=pltpu.HBM)
ANY = pl.BlockSpec(memory_space=pl.ANY)


def even_half(lanes):
    return lax.broadcasted_iota(jnp.int32, (SUB, lanes), 0) % 2 == 0


def flip_lanes(values):
    index = LANES - 1 - lax.broadcasted_iota(jnp.int32, (SUB, LANES), 1)
    chunks = range(0, values.shape[-1], LANES)
    parts = [jnp.take_along_axis(values[:, c : c + LANES], index, axis=1) for c in reversed(chunks)]
    return jnp.concatenate(parts, axis=1)


def run_copies(copies):
    for copy in copies:
        copy.start()
    for copy in copies:
        copy.wait()


def columns_kernel(vel, thick, trac, mask, out_a, out_b, edges, land, sem):
    levels, rows, width = thick.shape
    half_rows = rows // 2
    copies = []
    for side in range(2):
        lanes = pl.ds(side * (width - LANES), LANES)
        to = pl.ds(side * LANES, LANES)
        for level in range(levels):
            for half in range(2):
                at, s = pl.ds(half * half_rows, half_rows), 2 * level + half
                for source, target in (
                    (vel.at[:, level, at, lanes], edges.at[0:2, :, s, to]),
                    (thick.at[level, at, lanes], edges.at[2, :, s, to]),
                    (trac.at[:, level, at, lanes], edges.at[3:5, :, s, to]),
                    (mask.at[level, at, lanes], land.at[:, s, to]),
                ):
                    copies.append(pltpu.make_async_copy(source, target, sem))
    run_copies(copies)
    lon_even = lax.axis_index("lon") % 2 == 0
    group = lax.broadcasted_iota(jnp.int32, (SUB, LANES), 1) // HALO
    for f in range(6):
        west = east = jnp.zeros((SUB, LANES), F32)
        for row in range(half_rows):
            pair = edges[f, row] if f < 5 else land[row].astype(F32)
            here = group == row
            west = jnp.where(here, pltpu.roll(pair[:, :LANES], HALO * row % LANES, 1), west)
            east = jnp.where(here, pltpu.roll(pair[:, LANES:], HALO * (row + 1) % LANES, 1), east)
        out_a[f] = jnp.where(lon_even, east, west)
        out_b[f] = jnp.where(lon_even, west, east)


def load_kernel(lat_count, vel, thick, trac, mask, after, planes, coriolis, land, sem):
    del after
    levels, rows, width = thick.shape
    half_rows = rows // 2
    length = half_rows + PAD
    copies = []
    for level in range(levels):
        for half in range(2):
            at, s = pl.ds(half * (half_rows - PAD), length), 2 * level + half
            to = pl.ds((1 - half) * PAD, length)
            for source, target in (
                (vel.at[:, level, at, :], planes.at[0:2, to, s, :]),
                (thick.at[level, at, :], planes.at[2, to, s, :]),
                (trac.at[:, level, at, :], planes.at[3:5, to, s, :]),
                (mask.at[level, at, :], land.at[to, s, :]),
            ):
                copies.append(pltpu.make_async_copy(source, target, sem))
    for copy in copies:
        copy.start()
    total = rows * lat_count
    half = lax.broadcasted_iota(jnp.int32, (SUB, LANES), 0) % 2
    first = lax.axis_index("lat") * rows + half * half_rows
    for row in range(-2, half_rows + 2):
        ids = first + row
        folded = jnp.where(ids >= total, 2 * total - 1 - ids, ids)
        angle = jnp.pi * (folded.astype(F32) + 0.5) / total - jnp.pi / 2
        coriolis[row + PAD] = jnp.sin(angle)
    for copy in copies:
        copy.wait()
    for row in range(PAD - 2, half_rows + PAD + 2):
        planes[5, row] = land[row].astype(F32)


def halo_columns(cols_a, cols_b, lon_even):
    lane = lax.broadcasted_iota(jnp.int32, (SUB, LANES), 1)

    def get(f):
        a, b = cols_a[f], cols_b[f]
        from_west = jnp.where(lon_even, b, a)
        from_east = jnp.where(lon_even, a, b)

        def row(r):
            east = pltpu.roll(from_east, -HALO * r % LANES, 1)
            west = pltpu.roll(from_west, -HALO * (r + 1) % LANES, 1)
            return jnp.where(lane < LANES // 2, east, west)

        return row

    return get


def rows_kernel(lat_count, planes, cols_a, cols_b, out_a, out_b):
    half_rows, width = planes.shape[1] - 2 * PAD, planes.shape[3]
    chunks = width // LANES
    lat = lax.axis_index("lat")
    lat_even = lat % 2 == 0
    lon_even = lax.axis_index("lon") % 2 == 0
    even = even_half(width + LANES)
    group = lax.broadcasted_iota(jnp.int32, (SUB, LANES), 1) // 8
    get = halo_columns(cols_a, cols_b, lon_even)
    column = [get(f) for f in range(6)]
    slots = [(f, m) for f in range(5) for m in range(2)] + [(5, None)]

    def whole(f, row):
        return jnp.concatenate([planes[f, row + PAD], column[f](row)], axis=1)

    def north(f, m):
        low = half_rows - HALO + 2 * m
        return jnp.where(even, pltpu.roll(whole(f, low + 1), SUB - 1, 0), whole(f, low))

    def south(f, m):
        return jnp.where(even, whole(f, 2 * m), pltpu.roll(whole(f, 2 * m + 1), 1, 0))

    def put(target, slot, value):
        for c in range(chunks):
            target[chunks * slot + c] = value[:, c * LANES : (c + 1) * LANES]

    def add_corner(corner, slot, value):
        return jnp.where(group == slot, pltpu.roll(value[:, width:], 8 * slot + HALO, 1), corner)

    corner_a = corner_b = jnp.zeros((SUB, LANES), F32)
    for slot, (f, m) in enumerate(slots):
        to_north = north(f, 1 if m is None else m)
        to_south = south(f, 0 if m is None else m)
        a = jnp.where(lat_even, to_north, to_south)
        b = jnp.where(lat_even, to_south, to_north)
        put(out_a, slot, a)
        put(out_b, slot, b)
        corner_a = add_corner(corner_a, slot, a)
        corner_b = add_corner(corner_b, slot, b)
    out_a[chunks * SLOTS] = corner_a
    out_b[chunks * SLOTS] = corner_b

    @pl.when(lat == lat_count - 1)
    def _():
        target = out_a if (lat_count - 1) % 2 == 0 else out_b
        corner = jnp.zeros((SUB, LANES), F32)
        for slot, (f, m) in enumerate(slots):
            value = north(f, 1 if m is None else 1 - m)
            value = -value if f < 2 else value
            mirrored = jnp.concatenate([flip_lanes(value[:, :width]), flip_lanes(value[:, width:])], axis=1)
            put(target, slot, mirrored)
            corner = add_corner(corner, slot, mirrored)
        target[chunks * SLOTS] = corner


def make_step(wide, lap, east_diff, press):
    level = lax.broadcasted_iota(jnp.int32, (SUB, wide), 0) // 2
    weight = 1.0 / (level.astype(F32) + 1.0)
    below_one, below_two = level >= 1, level >= 2

    def shifts(value):
        return pltpu.roll(value, wide - 1, 1), pltpu.roll(value, 1, 1)

    def ahead(source, row):
        at = row + PAD
        centres = [source(f, row) for f in range(5)]
        for f in range(5):
            to_east, to_west = shifts(centres[f])
            lap[f, at] = (
                (to_east + to_west) + (source(f, row + 1) + source(f, row - 1)) - 4.0 * centres[f]
            )
            east_diff[f, at] = to_east - to_west
        part = weight * centres[2] + 0.1 * (0.8 * centres[4] - centres[3])
        part = part + jnp.where(below_one, pltpu.roll(part, 2, 0), 0.0)
        press[at] = part + jnp.where(below_two, pltpu.roll(part, 4, 0), 0.0)

    def update(source, ocean, coriolis, row, cut, emit):
        at = row + PAD
        lanes = slice(0, cut)
        u, v = source(0, row)[:, lanes], source(1, row)[:, lanes]
        half_u, half_v = (-0.5 * ADVECTION) * u, (-0.5 * ADVECTION) * v
        p_east, p_west = shifts(press[at])
        slope_east = (-0.5 * GRADIENT) * (p_east - p_west)[:, lanes]
        slope_north = (-0.5 * GRADIENT) * (press[at + 1, :, lanes] - press[at - 1, :, lanes])
        turn = jnp.concatenate([CORIOLIS * coriolis] * (cut // LANES), axis=1)
        for f in range(5):
            dx = east_diff[f, at, :, lanes]
            dy = source(f, row + 1)[:, lanes] - source(f, row - 1)[:, lanes]
            if f == 0:
                u_east = dx
            if f == 1:
                v_north = dy
            here = lap[f, at]
            l_east, l_west = shifts(here)
            around = (l_east + l_west)[:, lanes] + (
                lap[f, at + 1, :, lanes] + lap[f, at - 1, :, lanes]
            )
            value = source(f, row)[:, lanes] + (half_u * dx + half_v * dy)
            value = value + (
                (DIFFUSION + 4.0 * HYPERVISCOSITY) * here[:, lanes] - HYPERVISCOSITY * around
            )
            if f == 0:
                value = value + (turn * v + slope_east)
            if f == 1:
                value = value + (slope_north - turn * u)
            if f == 2:
                value = value - (0.5 * CONVERGENCE) * (u_east + v_north)
            emit(f, row, value * ocean)

    return ahead, update


def interior_kernel(planes, cols_a, cols_b, coriolis, after, out, ring, outer, second, lap, east_diff, press):
    del after
    half_rows, width = planes.shape[1] - 2 * PAD, planes.shape[3]
    wide = width + LANES
    lon_even = lax.axis_index("lon") % 2 == 0
    get = halo_columns(cols_a, cols_b, lon_even)
    for f in range(6):
        column = get(f)
        for row in range(half_rows):
            value = column(row)
            outer[f, row + PAD] = value
            if row < HALO:
                outer[f, row + PAD + half_rows] = pltpu.roll(value, SUB - 1, 0)
            if row >= half_rows - HALO:
                outer[f, row + PAD - half_rows] = pltpu.roll(value, 1, 0)
    ahead, update = make_step(wide, lap, east_diff, press)

    def whole(f, row):
        return jnp.concatenate([planes[f, row + PAD], outer[f, row + PAD]], axis=1)

    def keep(f, row, value):
        second[f, row + PAD] = value

    def halfway(f, row):
        return second[f, row + PAD]

    def write(f, row, value):
        out[f, row] = value

    def sweep(source, low, high, cut, emit):
        ahead(source, low - 1)
        ahead(source, low)

        def iteration(row, carry):
            ahead(source, row + 1)
            ocean = whole(5, row)[:, :cut]
            update(source, ocean, coriolis[row + PAD], row, cut, emit)
            return carry

        lax.fori_loop(low, high, iteration, 0)

    sweep(whole, 2, half_rows - 2, wide, keep)
    for f in range(5):
        for i in range(4):
            ring[f, i] = second[f, 2 + i + PAD]
            ring[f, 4 + i] = second[f, half_rows - 6 + i + PAD]
    sweep(halfway, HALO, half_rows - HALO, width, write)


def edges_kernel(
    planes, outer, coriolis, done, ring, rows_a, rows_b, vel_out, thick_out, trac_out, strip, second, lap, east_diff, press, sem
):
    half_rows, width = planes.shape[1] - 2 * PAD, planes.shape[3]
    wide = width + LANES
    chunks = width // LANES
    levels = SUB // 2

    def copies_out(source, source_row, row, count):
        copies = []
        for level in range(levels):
            for half in range(2):
                s = 2 * level + half
                rows, to = pl.ds(source_row, count), pl.ds(half * half_rows + row, count)
                copies += [
                    pltpu.make_async_copy(source.at[0:2, rows, s, :], vel_out.at[:, level, to, :], sem),
                    pltpu.make_async_copy(source.at[2, rows, s, :], thick_out.at[level, to, :], sem),
                    pltpu.make_async_copy(source.at[3:5, rows, s, :], trac_out.at[:, level, to, :], sem),
                ]
        for copy in copies:
            copy.start()
        return copies

    copies = copies_out(done, PAD, PAD, half_rows - 2 * PAD)
    for f in range(5):
        for i in range(HALO):
            strip[f, HALO + i] = done[f, HALO + i]
            strip[f, PAD + i] = done[f, half_rows - PAD + i]
    lat_even = lax.axis_index("lat") % 2 == 0
    even = even_half(wide)
    corner_a, corner_b = rows_a[chunks * SLOTS], rows_b[chunks * SLOTS]

    def message(ref, corner, slot):
        parts = [ref[chunks * slot + c] for c in range(chunks)]
        return jnp.concatenate([*parts, pltpu.roll(corner, -(8 * slot + HALO) % LANES, 1)], axis=1)

    south, north = {}, {}
    for f in range(6):
        reach = HALO if f < 5 else 2
        for m in range(reach // 2):
            slot = 2 * f + m
            a, b = message(rows_a, corner_a, slot), message(rows_b, corner_b, slot)
            from_south = jnp.where(lat_even, b, a)
            from_north = jnp.where(lat_even, a, b)
            south[f, 2 * m - reach] = pltpu.roll(from_south, SUB - 1, 0)
            south[f, 2 * m - reach + 1] = from_south
            north[f, half_rows + 2 * m] = pltpu.roll(from_north, 1, 0)
            north[f, half_rows + 2 * m + 1] = from_north

    def whole(f, row):
        own = jnp.concatenate([planes[f, row + PAD], outer[f, row + PAD]], axis=1)
        if row < 0:
            return jnp.where(even, south[f, row], own)
        if row >= half_rows:
            return jnp.where(even, own, north[f, row])
        return own

    ahead, update = make_step(wide, lap, east_diff, press)

    def halfway(f, row):
        if 2 <= row < 6:
            return ring[f, row - 2]
        if half_rows - 6 <= row < half_rows - 2:
            return ring[f, row - (half_rows - 6) + 4]
        return second[f, row + PAD]

    def keep(f, row, value):
        second[f, row + PAD] = value

    def write(f, row, value):
        strip[f, row if row < HALO else row - half_rows + 2 * PAD] = value

    def sweep(source, low, high, cut, emit):
        ahead(source, low - 1)
        ahead(source, low)
        for row in range(low, high):
            ahead(source, row + 1)
            update(source, whole(5, row)[:, :cut], coriolis[row + PAD], row, cut, emit)

    sweep(whole, -2, 2, wide, keep)
    sweep(halfway, 0, HALO, width, write)
    copies += copies_out(strip, 0, 0, PAD)
    sweep(whole, half_rows - 2, half_rows + 2, wide, keep)
    sweep(halfway, half_rows - HALO, half_rows, width, write)
    copies += copies_out(strip, PAD, half_rows - PAD, PAD)
    for copy in copies:
        copy.wait()


def lat_pairs(parity, lat_count, lon_count):
    pairs = []
    for lat in range(lat_count):
        for lon in range(lon_count):
            to_lat, to_lon = (lat + 1 if lat % 2 == parity else lat - 1), lon
            if to_lat < 0:
                continue
            if to_lat == lat_count:
                to_lat, to_lon = lat, lon_count - 1 - lon
            pairs.append((lon * lat_count + lat, to_lon * lat_count + to_lat))
    return pairs


def lon_pairs(parity, lon_count):
    return [(i, (i + 1 if i % 2 == parity else i - 1) % lon_count) for i in range(lon_count)]


def shapes(*dims):
    return jax.ShapeDtypeStruct(dims, F32)


def body(lat_count, lon_count, velocity, thickness, tracers, land_mask):
    levels, rows, width = thickness.shape
    half_rows = rows // 2
    wide, tall = width + LANES, half_rows + 2 * PAD
    fields = (velocity, thickness, tracers, land_mask)
    dma = pltpu.SemaphoreType.DMA

    def call(kernel, name, in_specs, outs, out_specs, scratch, flops):
        return pl.pallas_call(
            kernel,
            out_shape=outs,
            in_specs=in_specs,
            out_specs=out_specs,
            scratch_shapes=scratch,
            compiler_params=pltpu.CompilerParams(vmem_limit_bytes=40 * 2**20),
            cost_estimate=pl.CostEstimate(flops=flops, bytes_accessed=flops // 10, transcendentals=0),
            name=name,
        )

    columns = shapes(6, SUB, LANES)
    send_a, send_b = call(
        columns_kernel,
        "pack_columns",
        [HBM] * 4,
        (columns, columns),
        (VMEM, VMEM),
        [pltpu.VMEM((5, half_rows, SUB, 2 * LANES), F32), pltpu.VMEM((half_rows, SUB, 2 * LANES), jnp.int32), dma],
        10**6,
    )(*fields)
    cols_a = lax.ppermute(send_a, "lon", lon_pairs(0, lon_count))
    cols_b = lax.ppermute(send_b, "lon", lon_pairs(1, lon_count))

    planes, coriolis = call(
        functools.partial(load_kernel, lat_count),
        "load_fields",
        [HBM, HBM, HBM, HBM, ANY],
        (shapes(6, tall, SUB, width), shapes(tall, SUB, LANES)),
        (VMEM, VMEM),
        [pltpu.VMEM((tall, SUB, width), jnp.int32), dma],
        10**8,
    )(*fields, send_a)

    message = shapes(SLOTS * (width // LANES) + 1, SUB, LANES)
    send_a, send_b = call(
        functools.partial(rows_kernel, lat_count),
        "pack_rows",
        [VMEM] * 3,
        (message, message),
        (VMEM, VMEM),
        [],
        10**6,
    )(planes, cols_a, cols_b)
    axes = ("lon", "lat")
    rows_a = lax.ppermute(send_a, axes, lat_pairs(0, lat_count, lon_count))
    rows_b = lax.ppermute(send_b, axes, lat_pairs(1, lat_count, lon_count))

    wide_planes = pltpu.VMEM((5, tall, SUB, wide), F32)
    work = [wide_planes, wide_planes, wide_planes, pltpu.VMEM((tall, SUB, wide), F32)]
    done, ring, outer = call(
        interior_kernel,
        "interior",
        [VMEM, VMEM, VMEM, VMEM, ANY],
        (shapes(5, half_rows, SUB, width), shapes(5, 8, SUB, wide), shapes(6, tall, SUB, LANES)),
        (VMEM, VMEM, VMEM),
        work,
        10**8,
    )(planes, cols_a, cols_b, coriolis, send_a)

    return call(
        edges_kernel,
        "edges",
        [VMEM] * 7,
        (shapes(*velocity.shape), shapes(*thickness.shape), shapes(*tracers.shape)),
        (HBM, HBM, HBM),
        [pltpu.VMEM((5, 2 * PAD, SUB, width), F32), *work, dma],
        10**8,
    )(planes, outer, coriolis, done, ring, rows_a, rows_b)


def solution(mesh):
    specs = (P(None, None, "lat", "lon"), P(None, "lat", "lon"), P(None, None, "lat", "lon"))
    return jax.shard_map(
        functools.partial(body, mesh.shape["lat"], mesh.shape["lon"]),
        mesh=mesh,
        in_specs=(*specs, P(None, "lat", "lon")),
        out_specs=specs,
        check_vma=False,
    )
```

profile of v0, /device:TPU:0, one launch (start us, length us, event | category | flops | bytes accessed | tf_op | source)
XLA Modules:
  0.0 34.2 jit_solution(14278881063494714436)
XLA Ops:
  0.6 0.0 copy-start
  0.6 1.2 %copy-done = f32[2,4,64,512]{3,2,1,0:T(8,128)S(1)} copy-done((f32[2,4,64,512]{3,2,1,0:T(8,128)S(1)}, f32[2,4,64,512]{3,2,1,0:T(8,128)}, u32[]{:S(2)}) %copy-start) | copy-done | bytes 1048600
  1.9 0.0 copy-start.1
  1.9 1.2 %copy-done.1 = f32[2,4,64,512]{3,2,1,0:T(8,128)S(1)} copy-done((f32[2,4,64,512]{3,2,1,0:T(8,128)S(1)}, f32[2,4,64,512]{3,2,1,0:T(8,128)}, u32[]{:S(2)}) %copy-start.1) | copy-done | bytes 1048600
  3.1 0.0 copy-start.2
  3.1 1.0 %copy-done.2 = f32[4,64,512]{2,1,0:T(8,128)S(1)} copy-done((f32[4,64,512]{2,1,0:T(8,128)S(1)}, f32[4,64,512]{2,1,0:T(8,128)}, u32[]{:S(2)}) %copy-start.2) | copy-done | bytes 524312
  4.1 0.0 copy-start.3
  4.1 1.0 %copy-done.3 = s32[4,64,512]{2,1,0:T(8,128)S(1)} copy-done((s32[4,64,512]{2,1,0:T(8,128)S(1)}, s32[4,64,512]{2,1,0:T(8,128)}, u32[]{:S(2)}) %copy-start.3) | copy-done | bytes 524312
  5.2 1.6 %pack_columns.1 = (f32[6,8,128]{2,1,0:T(8,128)S(1)}, f32[6,8,128]{2,1,0:T(8,128)S(1)}) custom-call(f32[2,4,64,512]{3,2,1,0:T(8,128)S(1)} %copy-done, f32[4,64,512]{2,1,0:T(8,128)S(1)} %copy-done.2, f32[2,4,64,512]{3,2,1,0:T(8,128)S(1)} %copy-done.1, s32[4,64,512]{2,1,0:T(8,128)S(1)} %copy-done.3), custom_call_target="tpu_custom_call" | custom-call | flops 1000000 | bytes 100000 | tf_op jit(solution)/shard_map/pack_columns/pallas_call | solution.py:419
  6.8 3.4 %collective-permute-start.1 = (f32[6,8,128]{2,1,0:T(8,128)S(1)}, f32[6,8,128]{2,1,0:T(8,128)S(1)}, u32[]{:S(2)}, u32[]{:S(2)}) collective-permute-start(f32[6,8,128]{2,1,0:T(8,128)S(1)} %get-tuple-element.14), channel_id=1, source_target_pairs={{0,28},{4,8},{8,4},{12,16},{16,12},{20,24},{24,20},{28,0},{1,29},{... | collective-permute-start | bytes 73736 | tf_op jit(solution)/shard_map/ppermute | solution.py:429
  10.2 0.0 collective-permute-start
  10.2 3.4 %load_fields.1 = (f32[6,48,8,512]{3,2,1,0:T(8,128)S(1)}, f32[48,8,128]{2,1,0:T(8,128)S(1)}) custom-call(f32[2,4,64,512]{3,2,1,0:T(8,128)S(1)} %copy-done, f32[4,64,512]{2,1,0:T(8,128)S(1)} %copy-done.2, f32[2,4,64,512]{3,2,1,0:T(8,128)S(1)} %copy-done.1, s32[4,64,512]{2,1,0:T(8,128)S(1)} %copy-done.3, f32[6,8,128]{2,1,0:T(8,128)S(1)} %get-tuple-element.12.after), custom_call_target="tpu_custom_call" | custom-call | flops 100000000 | bytes 10000000 | tf_op jit(solution)/shard_map/load_fields/pallas_call | solution.py:431
  13.6 0.0 collective-permute-done.1.cols_b
  13.6 0.0 collective-permute-done.cols_a
  13.6 0.2 pack_rows.1
  13.8 0.7 %collective-permute-start.3 = (f32[45,8,128]{2,1,0:T(8,128)S(1)}, f32[45,8,128]{2,1,0:T(8,128)S(1)}, u32[]{:S(2)}, u32[]{:S(2)}) collective-permute-start(f32[45,8,128]{2,1,0:T(8,128)S(1)} %get-tuple-element.20), channel_id=1, source_target_pairs={{1,2},{5,6},{9,10},{13,14},{17,18},{21,22},{25,26},{29,30},{2,1},{... | collective-permute-start | bytes 552968 | tf_op jit(solution)/shard_map/ppermute | solution.py:453
  14.5 4.5 %collective-permute-start.2 = (f32[45,8,128]{2,1,0:T(8,128)S(1)}, f32[45,8,128]{2,1,0:T(8,128)S(1)}, u32[]{:S(2)}, u32[]{:S(2)}) collective-permute-start(f32[45,8,128]{2,1,0:T(8,128)S(1)} %get-tuple-element.16.after), channel_id=1, source_target_pairs={{0,1},{4,5},{8,9},{12,13},{16,17},{20,21},{24,25},{28,29},{1,0},{5... | collective-permute-start | bytes 552968 | tf_op jit(solution)/shard_map/ppermute | solution.py:452
  18.9 11.2 %interior.1 = (f32[5,32,8,512]{3,2,1,0:T(8,128)S(1)}, f32[5,8,8,640]{3,2,1,0:T(8,128)S(1)}, f32[6,48,8,128]{3,2,1,0:T(8,128)S(1)}) custom-call(f32[6,48,8,512]{3,2,1,0:T(8,128)S(1)} %get-tuple-element.13.planes, f32[6,8,128]{2,1,0:T(8,128)S(1)} %collective-permute-done.cols_a, f32[6,8,128]{2,1,0:T(8,128)S(1)} %collective-permute-done.1.cols_b, ...), custom_call_target="tpu_custom_call" | custom-call | flops 100000000 | bytes 10000000 | tf_op jit(solution)/shard_map/interior/pallas_call | solution.py:457
  30.2 0.0 collective-permute-done.3.rows_b
  30.2 0.0 collective-permute-done.2.rows_a
  30.2 4.0 %edges.1 = (f32[2,4,64,512]{3,2,1,0:T(8,128)}, f32[4,64,512]{2,1,0:T(8,128)}, f32[2,4,64,512]{3,2,1,0:T(8,128)}) custom-call(f32[6,48,8,512]{3,2,1,0:T(8,128)S(1)} %get-tuple-element.13.planes, f32[6,48,8,128]{3,2,1,0:T(8,128)S(1)} %get-tuple-element.17.outer, f32[48,8,128]{2,1,0:T(8,128)S(1)} %get-tuple-element.15.coriolis, ...), custom_call_target="tpu_custom_call" | custom-call | flops 100000000 | bytes 10000000 | tf_op jit(solution)/shard_map/edges/pallas_call | solution.py:467
Async XLA Ops:
  0.6 1.2 %copy-start = (f32[2,4,64,512]{3,2,1,0:T(8,128)S(1)}, f32[2,4,64,512]{3,2,1,0:T(8,128)}, u32[]{:S(2)}) copy-start(f32[2,4,64,512]{3,2,1,0:T(8,128)} %vel.3) | copy-start | bytes 3145732
  1.9 1.2 %copy-start.1 = (f32[2,4,64,512]{3,2,1,0:T(8,128)S(1)}, f32[2,4,64,512]{3,2,1,0:T(8,128)}, u32[]{:S(2)}) copy-start(f32[2,4,64,512]{3,2,1,0:T(8,128)} %trac.3) | copy-start | bytes 3145732
  3.1 1.0 %copy-start.2 = (f32[4,64,512]{2,1,0:T(8,128)S(1)}, f32[4,64,512]{2,1,0:T(8,128)}, u32[]{:S(2)}) copy-start(f32[4,64,512]{2,1,0:T(8,128)} %thick.3) | copy-start | bytes 1572868
  4.1 1.0 %copy-start.3 = (s32[4,64,512]{2,1,0:T(8,128)S(1)}, s32[4,64,512]{2,1,0:T(8,128)}, u32[]{:S(2)}) copy-start(s32[4,64,512]{2,1,0:T(8,128)} %mask.3) | copy-start | bytes 1572868
  6.8 6.8 %collective-permute-start.1 = (f32[6,8,128]{2,1,0:T(8,128)S(1)}, f32[6,8,128]{2,1,0:T(8,128)S(1)}, u32[]{:S(2)}, u32[]{:S(2)}) collective-permute-start(f32[6,8,128]{2,1,0:T(8,128)S(1)} %get-tuple-element.14), channel_id=1, source_target_pairs={{0,28},{4,8},{8,4},{12,16},{16,12},{20,24},{24,20},{28,0},{1,29},{... | collective-permute-start | bytes 73736 | tf_op jit(solution)/shard_map/ppermute | solution.py:429
  10.2 3.4 %collective-permute-start = (f32[6,8,128]{2,1,0:T(8,128)S(1)}, f32[6,8,128]{2,1,0:T(8,128)S(1)}, u32[]{:S(2)}, u32[]{:S(2)}) collective-permute-start(f32[6,8,128]{2,1,0:T(8,128)S(1)} %get-tuple-element.12.after), channel_id=1, source_target_pairs={{0,4},{4,0},{8,12},{12,8},{16,20},{20,16},{24,28},{28,24},{1,5},{5... | collective-permute-start | bytes 73736 | tf_op jit(solution)/shard_map/ppermute | solution.py:428
  13.8 16.3 %collective-permute-start.3 = (f32[45,8,128]{2,1,0:T(8,128)S(1)}, f32[45,8,128]{2,1,0:T(8,128)S(1)}, u32[]{:S(2)}, u32[]{:S(2)}) collective-permute-start(f32[45,8,128]{2,1,0:T(8,128)S(1)} %get-tuple-element.20), channel_id=1, source_target_pairs={{1,2},{5,6},{9,10},{13,14},{17,18},{21,22},{25,26},{29,30},{2,1},{... | collective-permute-start | bytes 552968 | tf_op jit(solution)/shard_map/ppermute | solution.py:453
  14.5 15.7 %collective-permute-start.2 = (f32[45,8,128]{2,1,0:T(8,128)S(1)}, f32[45,8,128]{2,1,0:T(8,128)S(1)}, u32[]{:S(2)}, u32[]{:S(2)}) collective-permute-start(f32[45,8,128]{2,1,0:T(8,128)S(1)} %get-tuple-element.16.after), channel_id=1, source_target_pairs={{0,1},{4,5},{8,9},{12,13},{16,17},{20,21},{24,25},{28,29},{1,0},{5... | collective-permute-start | bytes 552968 | tf_op jit(solution)/shard_map/ppermute | solution.py:452
where the time goes:
time: 34.5 us; the launch traced here: 34.2 us
  Pallas kernels  20.4 us (59%)
  starting transfers between devices  8.53 us (25%)
  local copies, waits for them, and re-layouts  4.52 us (13%)
  between operations  0.71 us (2%)
    pallas_call x1, Pallas kernels, body(): call(interior_kernel, 'interior', [VMEM, VMEM, VMEM, VMEM, ANY], (shapes(...  11.2 us
    unnamed x8, local copies, waits for them, and re-layouts  4.52 us
    ppermute x1, starting transfers between devices, body(): rows_a = lax.ppermute(send_a, axes, lat_pairs(0, lat_count, lon_count))  4.45 us
    pallas_call x1, Pallas kernels, body(): call(edges_kernel, 'edges', [VMEM] * 7, (shapes(*velocity.shape), shapes(...  4.01 us
    ppermute x1, starting transfers between devices, body(): cols_b = lax.ppermute(send_b, 'lon', lon_pairs(1, lon_count))  3.4 us
    pallas_call x1, Pallas kernels, body(): call(functools.partial(load_kernel, lat_count), 'load_fields', [HBM, HBM,...  3.39 us
    pallas_call x1, Pallas kernels, body(): call(columns_kernel, 'pack_columns', [HBM] * 4, (columns, columns), (VMEM...  1.58 us
  transfers between devices with their start and end apart: 4, of which 0 were waited for; matrix products, arithmetic and copies ran while one was open for 0% of the time, Pallas kernels for 43%

commit v1 on v0

--- a/solution.py
+++ b/solution.py
@@ -400,7 +400,8 @@
     levels, rows, width = thickness.shape
     half_rows = rows // 2
     wide, tall = width + LANES, half_rows + 2 * PAD
-    fields = (velocity, thickness, tracers, land_mask)
+    arguments = (velocity, thickness, tracers, land_mask)
+    fields = [pltpu.with_memory_space_constraint(x, pltpu.HBM) for x in arguments]
     dma = pltpu.SemaphoreType.DMA
 
     def call(kernel, name, in_specs, outs, out_specs, scratch, flops):

time: 34.5 us -> 29.2 us (0.85)
  local copies, waits for them, and re-layouts: 4.52 us -> 0 us
  Pallas kernels: 20.4 us -> 19.6 us
    unnamed x8 -> x0, local copies, waits for them, and re-layouts: 4.52 us -> none
    pallas_call x1, Pallas kernels: 3.39 us -> 2.26 us  [body(): call(functools.partial(load_kernel, lat_count), 'load_fields', [HBM, HBM,...]
  transfers between devices with their start and end apart: 4 -> 4, of which waited for: 0 -> 0; matrix products, arithmetic and copies ran while one was open for 0% -> 0% of each run, Pallas kernels for 43% -> 46%
where the time goes in v1:
time: 29.2 us; the launch traced here: 29 us
  Pallas kernels  19.6 us (67%)
  starting transfers between devices  8.67 us (30%)
  between operations  0.69 us (2%)
    pallas_call x1, Pallas kernels, body(): call(interior_kernel, 'interior', [VMEM, VMEM, VMEM, VMEM, ANY], (shapes(...  11.2 us
    ppermute x1, starting transfers between devices, body(): rows_a = lax.ppermute(send_a, axes, lat_pairs(0, lat_count, lon_count))  4.59 us
    pallas_call x1, Pallas kernels, body(): call(edges_kernel, 'edges', [VMEM] * 7, (shapes(*velocity.shape), shapes(...  4.01 us
    ppermute x1, starting transfers between devices, body(): cols_b = lax.ppermute(send_b, 'lon', lon_pairs(1, lon_count))  3.4 us
    pallas_call x1, Pallas kernels, body(): call(functools.partial(load_kernel, lat_count), 'load_fields', [HBM, HBM,...  2.26 us
    pallas_call x1, Pallas kernels, body(): call(columns_kernel, 'pack_columns', [HBM] * 4, (columns, columns), (VMEM...  1.88 us
    ppermute x1, starting transfers between devices, body(): rows_b = lax.ppermute(send_b, axes, lat_pairs(1, lat_count, lon_count))  0.67 us
  transfers between devices with their start and end apart: 4, of which 0 were waited for; matrix products, arithmetic and copies ran while one was open for 0% of the time, Pallas kernels for 46%

profile of v1, /device:TPU:0, one launch (start us, length us, event | category | flops | bytes accessed | tf_op | source)
XLA Modules:
  0.0 29.0 jit_solution(15666142157630032961)
XLA Ops:
  0.6 1.9 %pack_columns.1 = (f32[6,8,128]{2,1,0:T(8,128)S(1)}, f32[6,8,128]{2,1,0:T(8,128)S(1)}) custom-call(f32[2,4,64,512]{3,2,1,0:T(8,128)} %vel.3, f32[4,64,512]{2,1,0:T(8,128)} %thick.3, f32[2,4,64,512]{3,2,1,0:T(8,128)} %trac.3, s32[4,64,512]{2,1,0:T(8,128)} %mask.3), custom_call_target="tpu_custom_call" | custom-call | flops 1000000 | bytes 100000 | tf_op jit(solution)/shard_map/pack_columns/pallas_call | solution.py:420
  2.5 3.4 %collective-permute-start.1 = (f32[6,8,128]{2,1,0:T(8,128)S(1)}, f32[6,8,128]{2,1,0:T(8,128)S(1)}, u32[]{:S(2)}, u32[]{:S(2)}) collective-permute-start(f32[6,8,128]{2,1,0:T(8,128)S(1)} %get-tuple-element.14), channel_id=1, source_target_pairs={{0,28},{4,8},{8,4},{12,16},{16,12},{20,24},{24,20},{28,0},{1,29},{... | collective-permute-start | bytes 73736 | tf_op jit(solution)/shard_map/ppermute | solution.py:430
  5.9 0.0 collective-permute-start
  5.9 2.3 %load_fields.1 = (f32[6,48,8,512]{3,2,1,0:T(8,128)S(1)}, f32[48,8,128]{2,1,0:T(8,128)S(1)}) custom-call(f32[2,4,64,512]{3,2,1,0:T(8,128)} %vel.3, f32[4,64,512]{2,1,0:T(8,128)} %thick.3, f32[2,4,64,512]{3,2,1,0:T(8,128)} %trac.3, s32[4,64,512]{2,1,0:T(8,128)} %mask.3, f32[6,8,128]{2,1,0:T(8,128)S(1)} %get-tuple-element.12.after), custom_call_target="tpu_custom_call" | custom-call | flops 100000000 | bytes 10000000 | tf_op jit(solution)/shard_map/load_fields/pallas_call | solution.py:432
  8.2 0.0 collective-permute-done.1.cols_b
  8.2 0.0 collective-permute-done.cols_a
  8.2 0.2 pack_rows.1
  8.4 0.7 %collective-permute-start.3 = (f32[45,8,128]{2,1,0:T(8,128)S(1)}, f32[45,8,128]{2,1,0:T(8,128)S(1)}, u32[]{:S(2)}, u32[]{:S(2)}) collective-permute-start(f32[45,8,128]{2,1,0:T(8,128)S(1)} %get-tuple-element.20), channel_id=1, source_target_pairs={{1,2},{5,6},{9,10},{13,14},{17,18},{21,22},{25,26},{29,30},{2,1},{... | collective-permute-start | bytes 552968 | tf_op jit(solution)/shard_map/ppermute | solution.py:454
  9.1 4.6 %collective-permute-start.2 = (f32[45,8,128]{2,1,0:T(8,128)S(1)}, f32[45,8,128]{2,1,0:T(8,128)S(1)}, u32[]{:S(2)}, u32[]{:S(2)}) collective-permute-start(f32[45,8,128]{2,1,0:T(8,128)S(1)} %get-tuple-element.16.after), channel_id=1, source_target_pairs={{0,1},{4,5},{8,9},{12,13},{16,17},{20,21},{24,25},{28,29},{1,0},{5... | collective-permute-start | bytes 552968 | tf_op jit(solution)/shard_map/ppermute | solution.py:453
  13.7 11.2 %interior.1 = (f32[5,32,8,512]{3,2,1,0:T(8,128)S(1)}, f32[5,8,8,640]{3,2,1,0:T(8,128)S(1)}, f32[6,48,8,128]{3,2,1,0:T(8,128)S(1)}) custom-call(f32[6,48,8,512]{3,2,1,0:T(8,128)S(1)} %get-tuple-element.13.planes, f32[6,8,128]{2,1,0:T(8,128)S(1)} %collective-permute-done.cols_a, f32[6,8,128]{2,1,0:T(8,128)S(1)} %collective-permute-done.1.cols_b, ...), custom_call_target="tpu_custom_call" | custom-call | flops 100000000 | bytes 10000000 | tf_op jit(solution)/shard_map/interior/pallas_call | solution.py:458
  24.9 0.0 collective-permute-done.3.rows_b
  24.9 0.0 collective-permute-done.2.rows_a
  24.9 4.0 %edges.1 = (f32[2,4,64,512]{3,2,1,0:T(8,128)}, f32[4,64,512]{2,1,0:T(8,128)}, f32[2,4,64,512]{3,2,1,0:T(8,128)}) custom-call(f32[6,48,8,512]{3,2,1,0:T(8,128)S(1)} %get-tuple-element.13.planes, f32[6,48,8,128]{3,2,1,0:T(8,128)S(1)} %get-tuple-element.17.outer, f32[48,8,128]{2,1,0:T(8,128)S(1)} %get-tuple-element.15.coriolis, ...), custom_call_target="tpu_custom_call" | custom-call | flops 100000000 | bytes 10000000 | tf_op jit(solution)/shard_map/edges/pallas_call | solution.py:468
Async XLA Ops:
  2.5 5.7 %collective-permute-start.1 = (f32[6,8,128]{2,1,0:T(8,128)S(1)}, f32[6,8,128]{2,1,0:T(8,128)S(1)}, u32[]{:S(2)}, u32[]{:S(2)}) collective-permute-start(f32[6,8,128]{2,1,0:T(8,128)S(1)} %get-tuple-element.14), channel_id=1, source_target_pairs={{0,28},{4,8},{8,4},{12,16},{16,12},{20,24},{24,20},{28,0},{1,29},{... | collective-permute-start | bytes 73736 | tf_op jit(solution)/shard_map/ppermute | solution.py:430
  5.9 2.3 %collective-permute-start = (f32[6,8,128]{2,1,0:T(8,128)S(1)}, f32[6,8,128]{2,1,0:T(8,128)S(1)}, u32[]{:S(2)}, u32[]{:S(2)}) collective-permute-start(f32[6,8,128]{2,1,0:T(8,128)S(1)} %get-tuple-element.12.after), channel_id=1, source_target_pairs={{0,4},{4,0},{8,12},{12,8},{16,20},{20,16},{24,28},{28,24},{1,5},{5... | collective-permute-start | bytes 73736 | tf_op jit(solution)/shard_map/ppermute | solution.py:429
  8.4 16.5 %collective-permute-start.3 = (f32[45,8,128]{2,1,0:T(8,128)S(1)}, f32[45,8,128]{2,1,0:T(8,128)S(1)}, u32[]{:S(2)}, u32[]{:S(2)}) collective-permute-start(f32[45,8,128]{2,1,0:T(8,128)S(1)} %get-tuple-element.20), channel_id=1, source_target_pairs={{1,2},{5,6},{9,10},{13,14},{17,18},{21,22},{25,26},{29,30},{2,1},{... | collective-permute-start | bytes 552968 | tf_op jit(solution)/shard_map/ppermute | solution.py:454
  9.1 15.8 %collective-permute-start.2 = (f32[45,8,128]{2,1,0:T(8,128)S(1)}, f32[45,8,128]{2,1,0:T(8,128)S(1)}, u32[]{:S(2)}, u32[]{:S(2)}) collective-permute-start(f32[45,8,128]{2,1,0:T(8,128)S(1)} %get-tuple-element.16.after), channel_id=1, source_target_pairs={{0,1},{4,5},{8,9},{12,13},{16,17},{20,21},{24,25},{28,29},{1,0},{5... | collective-permute-start | bytes 552968 | tf_op jit(solution)/shard_map/ppermute | solution.py:453

commit v2 on v1

--- a/solution.py
+++ b/solution.py
@@ -276,7 +276,7 @@
             update(source, ocean, coriolis[row + PAD], row, cut, emit)
             return carry
 
-        lax.fori_loop(low, high, iteration, 0)
+        lax.fori_loop(low, high, iteration, 0, unroll=4)
 
     sweep(whole, 2, half_rows - 2, wide, keep)
     for f in range(5):
@@ -314,7 +314,8 @@
         for i in range(HALO):
             strip[f, HALO + i] = done[f, HALO + i]
             strip[f, PAD + i] = done[f, half_rows - PAD + i]
-    lat_even = lax.axis_index("lat") % 2 == 0
+    lat = lax.axis_index("lat")
+    lat_even, southmost = lat % 2 == 0, lat == 0
     even = even_half(wide)
     corner_a, corner_b = rows_a[chunks * SLOTS], rows_b[chunks * SLOTS]
 
@@ -328,7 +329,7 @@
         for m in range(reach // 2):
             slot = 2 * f + m
             a, b = message(rows_a, corner_a, slot), message(rows_b, corner_b, slot)
-            from_south = jnp.where(lat_even, b, a)
+            from_south = jnp.where(southmost, 0.0, jnp.where(lat_even, b, a))
             from_north = jnp.where(lat_even, a, b)
             south[f, 2 * m - reach] = pltpu.roll(from_south, SUB - 1, 0)
             south[f, 2 * m - reach + 1] = from_south
@@ -381,7 +382,7 @@
         for lon in range(lon_count):
             to_lat, to_lon = (lat + 1 if lat % 2 == parity else lat - 1), lon
             if to_lat < 0:
-                continue
+                to_lat, to_lon = 0, lon ^ 1
             if to_lat == lat_count:
                 to_lat, to_lon = lat, lon_count - 1 - lon
             pairs.append((lon * lat_count + lat, to_lon * lat_count + to_lat))

time: 29.2 us -> 24.1 us (0.83)
  Pallas kernels: 19.6 us -> 16.4 us
  starting transfers between devices: 8.67 us -> 6.76 us
    pallas_call x1, Pallas kernels: 11.2 us -> 8.03 us  [body(): call(interior_kernel, 'interior', [VMEM, VMEM, VMEM, VMEM, ANY], (shapes(...]
    ppermute x1, starting transfers between devices: 4.59 us -> 2.79 us  [body(): rows_a = lax.ppermute(send_a, axes, lat_pairs(0, lat_count, lon_count))]
  transfers between devices with their start and end apart: 4 -> 4, of which waited for: 0 -> 0; matrix products, arithmetic and copies ran while one was open for 0% -> 0% of each run, Pallas kernels for 46% -> 43%
where the time goes in v2:
time: 24.1 us; the launch traced here: 23.9 us
  Pallas kernels  16.4 us (68%)
  starting transfers between devices  6.76 us (28%)
  between operations  0.69 us (3%)
    pallas_call x1, Pallas kernels, body(): call(interior_kernel, 'interior', [VMEM, VMEM, VMEM, VMEM, ANY], (shapes(...  8.03 us
    pallas_call x1, Pallas kernels, body(): call(edges_kernel, 'edges', [VMEM] * 7, (shapes(*velocity.shape), shapes(...  4 us
    ppermute x1, starting transfers between devices, body(): cols_b = lax.ppermute(send_b, 'lon', lon_pairs(1, lon_count))  3.4 us
    ppermute x1, starting transfers between devices, body(): rows_a = lax.ppermute(send_a, axes, lat_pairs(0, lat_count, lon_count))  2.79 us
    pallas_call x1, Pallas kernels, body(): call(functools.partial(load_kernel, lat_count), 'load_fields', [HBM, HBM,...  2.26 us
    pallas_call x1, Pallas kernels, body(): call(columns_kernel, 'pack_columns', [HBM] * 4, (columns, columns), (VMEM...  1.88 us
    ppermute x1, starting transfers between devices, body(): rows_b = lax.ppermute(send_b, axes, lat_pairs(1, lat_count, lon_count))  0.56 us
  transfers between devices with their start and end apart: 4, of which 0 were waited for; matrix products, arithmetic and copies ran while one was open for 0% of the time, Pallas kernels for 43%

profile of v2, /device:TPU:0, one launch (start us, length us, event | category | flops | bytes accessed | tf_op | source)
XLA Modules:
  0.0 23.9 jit_solution(17929909467200738408)
XLA Ops:
  0.6 1.9 %pack_columns.1 = (f32[6,8,128]{2,1,0:T(8,128)S(1)}, f32[6,8,128]{2,1,0:T(8,128)S(1)}) custom-call(f32[2,4,64,512]{3,2,1,0:T(8,128)} %vel.3, f32[4,64,512]{2,1,0:T(8,128)} %thick.3, f32[2,4,64,512]{3,2,1,0:T(8,128)} %trac.3, s32[4,64,512]{2,1,0:T(8,128)} %mask.3), custom_call_target="tpu_custom_call" | custom-call | flops 1000000 | bytes 100000 | tf_op jit(solution)/shard_map/pack_columns/pallas_call | solution.py:421
  2.5 3.4 %collective-permute-start.1 = (f32[6,8,128]{2,1,0:T(8,128)S(1)}, f32[6,8,128]{2,1,0:T(8,128)S(1)}, u32[]{:S(2)}, u32[]{:S(2)}) collective-permute-start(f32[6,8,128]{2,1,0:T(8,128)S(1)} %get-tuple-element.14), channel_id=1, source_target_pairs={{0,28},{4,8},{8,4},{12,16},{16,12},{20,24},{24,20},{28,0},{1,29},{... | collective-permute-start | bytes 73736 | tf_op jit(solution)/shard_map/ppermute | solution.py:431
  5.9 0.0 collective-permute-start
  5.9 2.3 %load_fields.1 = (f32[6,48,8,512]{3,2,1,0:T(8,128)S(1)}, f32[48,8,128]{2,1,0:T(8,128)S(1)}) custom-call(f32[2,4,64,512]{3,2,1,0:T(8,128)} %vel.3, f32[4,64,512]{2,1,0:T(8,128)} %thick.3, f32[2,4,64,512]{3,2,1,0:T(8,128)} %trac.3, s32[4,64,512]{2,1,0:T(8,128)} %mask.3, f32[6,8,128]{2,1,0:T(8,128)S(1)} %get-tuple-element.12.after), custom_call_target="tpu_custom_call" | custom-call | flops 100000000 | bytes 10000000 | tf_op jit(solution)/shard_map/load_fields/pallas_call | solution.py:433
  8.2 0.0 collective-permute-done.1.cols_b
  8.2 0.0 collective-permute-done.cols_a
  8.2 0.2 pack_rows.1
  8.4 0.6 %collective-permute-start.3 = (f32[45,8,128]{2,1,0:T(8,128)S(1)}, f32[45,8,128]{2,1,0:T(8,128)S(1)}, u32[]{:S(2)}, u32[]{:S(2)}) collective-permute-start(f32[45,8,128]{2,1,0:T(8,128)S(1)} %get-tuple-element.20), channel_id=1, source_target_pairs={{0,4},{4,0},{8,12},{12,8},{16,20},{20,16},{24,28},{28,24},{1,2},{5... | collective-permute-start | bytes 552968 | tf_op jit(solution)/shard_map/ppermute | solution.py:455
  9.0 2.8 %collective-permute-start.2 = (f32[45,8,128]{2,1,0:T(8,128)S(1)}, f32[45,8,128]{2,1,0:T(8,128)S(1)}, u32[]{:S(2)}, u32[]{:S(2)}) collective-permute-start(f32[45,8,128]{2,1,0:T(8,128)S(1)} %get-tuple-element.16.after), channel_id=1, source_target_pairs={{0,1},{4,5},{8,9},{12,13},{16,17},{20,21},{24,25},{28,29},{1,0},{5... | collective-permute-start | bytes 552968 | tf_op jit(solution)/shard_map/ppermute | solution.py:454
  11.8 8.0 %interior.1 = (f32[5,32,8,512]{3,2,1,0:T(8,128)S(1)}, f32[5,8,8,640]{3,2,1,0:T(8,128)S(1)}, f32[6,48,8,128]{3,2,1,0:T(8,128)S(1)}) custom-call(f32[6,48,8,512]{3,2,1,0:T(8,128)S(1)} %get-tuple-element.13.planes, f32[6,8,128]{2,1,0:T(8,128)S(1)} %collective-permute-done.cols_a, f32[6,8,128]{2,1,0:T(8,128)S(1)} %collective-permute-done.1.cols_b, ...), custom_call_target="tpu_custom_call" | custom-call | flops 100000000 | bytes 10000000 | tf_op jit(solution)/shard_map/interior/pallas_call | solution.py:459
  19.8 0.0 collective-permute-done.3.rows_b
  19.8 0.0 collective-permute-done.2.rows_a
  19.9 4.0 %edges.1 = (f32[2,4,64,512]{3,2,1,0:T(8,128)}, f32[4,64,512]{2,1,0:T(8,128)}, f32[2,4,64,512]{3,2,1,0:T(8,128)}) custom-call(f32[6,48,8,512]{3,2,1,0:T(8,128)S(1)} %get-tuple-element.13.planes, f32[6,48,8,128]{3,2,1,0:T(8,128)S(1)} %get-tuple-element.17.outer, f32[48,8,128]{2,1,0:T(8,128)S(1)} %get-tuple-element.15.coriolis, ...), custom_call_target="tpu_custom_call" | custom-call | flops 100000000 | bytes 10000000 | tf_op jit(solution)/shard_map/edges/pallas_call | solution.py:469
Async XLA Ops:
  2.5 5.7 %collective-permute-start.1 = (f32[6,8,128]{2,1,0:T(8,128)S(1)}, f32[6,8,128]{2,1,0:T(8,128)S(1)}, u32[]{:S(2)}, u32[]{:S(2)}) collective-permute-start(f32[6,8,128]{2,1,0:T(8,128)S(1)} %get-tuple-element.14), channel_id=1, source_target_pairs={{0,28},{4,8},{8,4},{12,16},{16,12},{20,24},{24,20},{28,0},{1,29},{... | collective-permute-start | bytes 73736 | tf_op jit(solution)/shard_map/ppermute | solution.py:431
  5.9 2.3 %collective-permute-start = (f32[6,8,128]{2,1,0:T(8,128)S(1)}, f32[6,8,128]{2,1,0:T(8,128)S(1)}, u32[]{:S(2)}, u32[]{:S(2)}) collective-permute-start(f32[6,8,128]{2,1,0:T(8,128)S(1)} %get-tuple-element.12.after), channel_id=1, source_target_pairs={{0,4},{4,0},{8,12},{12,8},{16,20},{20,16},{24,28},{28,24},{1,5},{5... | collective-permute-start | bytes 73736 | tf_op jit(solution)/shard_map/ppermute | solution.py:430
  8.4 11.4 %collective-permute-start.3 = (f32[45,8,128]{2,1,0:T(8,128)S(1)}, f32[45,8,128]{2,1,0:T(8,128)S(1)}, u32[]{:S(2)}, u32[]{:S(2)}) collective-permute-start(f32[45,8,128]{2,1,0:T(8,128)S(1)} %get-tuple-element.20), channel_id=1, source_target_pairs={{0,4},{4,0},{8,12},{12,8},{16,20},{20,16},{24,28},{28,24},{1,2},{5... | collective-permute-start | bytes 552968 | tf_op jit(solution)/shard_map/ppermute | solution.py:455
  9.0 10.8 %collective-permute-start.2 = (f32[45,8,128]{2,1,0:T(8,128)S(1)}, f32[45,8,128]{2,1,0:T(8,128)S(1)}, u32[]{:S(2)}, u32[]{:S(2)}) collective-permute-start(f32[45,8,128]{2,1,0:T(8,128)S(1)} %get-tuple-element.16.after), channel_id=1, source_target_pairs={{0,1},{4,5},{8,9},{12,13},{16,17},{20,21},{24,25},{28,29},{1,0},{5... | collective-permute-start | bytes 552968 | tf_op jit(solution)/shard_map/ppermute | solution.py:454

commit v3 on v2

--- a/solution.py
+++ b/solution.py
@@ -66,7 +66,7 @@
     for f in range(6):
         west = east = jnp.zeros((SUB, LANES), F32)
         for row in range(half_rows):
-            pair = edges[f, row] if f < 5 else land[row].astype(F32)
+            pair = edges[f, row] if f < 5 else HYPERVISCOSITY * land[row].astype(F32)
             here = group == row
             west = jnp.where(here, pltpu.roll(pair[:, :LANES], HALO * row % LANES, 1), west)
             east = jnp.where(here, pltpu.roll(pair[:, LANES:], HALO * (row + 1) % LANES, 1), east)
@@ -100,11 +100,11 @@
         ids = first + row
         folded = jnp.where(ids >= total, 2 * total - 1 - ids, ids)
         angle = jnp.pi * (folded.astype(F32) + 0.5) / total - jnp.pi / 2
-        coriolis[row + PAD] = jnp.sin(angle)
+        coriolis[row + PAD] = (CORIOLIS / HYPERVISCOSITY) * jnp.sin(angle)
     for copy in copies:
         copy.wait()
     for row in range(PAD - 2, half_rows + PAD + 2):
-        planes[5, row] = land[row].astype(F32)
+        planes[5, row] = HYPERVISCOSITY * land[row].astype(F32)
 
 
 def halo_columns(cols_a, cols_b, lon_even):
@@ -180,66 +180,94 @@
         target[chunks * SLOTS] = corner
 
 
-def make_step(wide, lap, east_diff, press):
+def make_step(wide, sums, east_diff, press):
+    scale = 1.0 / HYPERVISCOSITY
+    keep_own = scale * (1.0 - 4.0 * DIFFUSION - 16.0 * HYPERVISCOSITY)
+    keep_sum = scale * (DIFFUSION + 8.0 * HYPERVISCOSITY)
+    advect = -0.5 * ADVECTION * scale
+    slope = -0.5 * GRADIENT * scale
+    converge = -0.5 * CONVERGENCE * scale
     level = lax.broadcasted_iota(jnp.int32, (SUB, wide), 0) // 2
-    weight = 1.0 / (level.astype(F32) + 1.0)
+    weight = slope / (level.astype(F32) + 1.0)
     below_one, below_two = level >= 1, level >= 2
 
     def shifts(value):
         return pltpu.roll(value, wide - 1, 1), pltpu.roll(value, 1, 1)
 
-    def ahead(source, row):
-        at = row + PAD
-        centres = [source(f, row) for f in range(5)]
-        for f in range(5):
-            to_east, to_west = shifts(centres[f])
-            lap[f, at] = (
-                (to_east + to_west) + (source(f, row + 1) + source(f, row - 1)) - 4.0 * centres[f]
-            )
-            east_diff[f, at] = to_east - to_west
-        part = weight * centres[2] + 0.1 * (0.8 * centres[4] - centres[3])
+    def ahead(source, row, at, f):
+        to_east, to_west = shifts(source(f, row))
+        sums[f, at] = (to_east + to_west) + (source(f, row + 1) + source(f, row - 1))
+        east_diff[f, at] = to_east - to_west
+
+    def ahead_press(source, row, at):
+        part = weight * source(2, row) + ((0.08 * slope) * source(4, row) - (0.1 * slope) * source(3, row))
         part = part + jnp.where(below_one, pltpu.roll(part, 2, 0), 0.0)
         press[at] = part + jnp.where(below_two, pltpu.roll(part, 4, 0), 0.0)
 
-    def update(source, ocean, coriolis, row, cut, emit):
-        at = row + PAD
+    def update(source, ocean, turn, row, at, cut, emit, northward):
         lanes = slice(0, cut)
+        turn = jnp.concatenate([turn] * (cut // LANES), axis=1)
         u, v = source(0, row)[:, lanes], source(1, row)[:, lanes]
-        half_u, half_v = (-0.5 * ADVECTION) * u, (-0.5 * ADVECTION) * v
-        p_east, p_west = shifts(press[at])
-        slope_east = (-0.5 * GRADIENT) * (p_east - p_west)[:, lanes]
-        slope_north = (-0.5 * GRADIENT) * (press[at + 1, :, lanes] - press[at - 1, :, lanes])
-        turn = jnp.concatenate([CORIOLIS * coriolis] * (cut // LANES), axis=1)
-        for f in range(5):
+        along_u, along_v = advect * u, advect * v
+        if northward is not None:
+            along_v = along_v * northward[:, lanes]
+
+        def add_on(f):
+            if f == 0:
+                p_east, p_west = shifts(press[at])
+                return turn * v + (p_east - p_west)[:, lanes]
+            if f == 1:
+                rise = press[at + 1, :, lanes] - press[at - 1, :, lanes]
+                if northward is not None:
+                    rise = rise * northward[:, lanes]
+                return rise - turn * u
+            v_north = source(1, row + 1)[:, lanes] - source(1, row - 1)[:, lanes]
+            if northward is not None:
+                v_north = v_north * northward[:, lanes]
+            return converge * (east_diff[0, at, :, lanes] + v_north)
+
+        def one(f):
+            here = sums[f, at]
+            s_east, s_west = shifts(here)
+            around = (s_east + s_west)[:, lanes] + (sums[f, at + 1, :, lanes] + sums[f, at - 1, :, lanes])
             dx = east_diff[f, at, :, lanes]
             dy = source(f, row + 1)[:, lanes] - source(f, row - 1)[:, lanes]
-            if f == 0:
-                u_east = dx
-            if f == 1:
-                v_north = dy
-            here = lap[f, at]
-            l_east, l_west = shifts(here)
-            around = (l_east + l_west)[:, lanes] + (
-                lap[f, at + 1, :, lanes] + lap[f, at - 1, :, lanes]
-            )
-            value = source(f, row)[:, lanes] + (half_u * dx + half_v * dy)
-            value = value + (
-                (DIFFUSION + 4.0 * HYPERVISCOSITY) * here[:, lanes] - HYPERVISCOSITY * around
-            )
-            if f == 0:
-                value = value + (turn * v + slope_east)
-            if f == 1:
-                value = value + (slope_north - turn * u)
-            if f == 2:
-                value = value - (0.5 * CONVERGENCE) * (u_east + v_north)
+            value = keep_own * source(f, row)[:, lanes] + (keep_sum * here[:, lanes] - around)
+            value = value + (along_u * dx + along_v * dy)
+            if f < 3:
+                value = value + add_on(f)
             emit(f, row, value * ocean)
 
-    return ahead, update
-
-
-def interior_kernel(planes, cols_a, cols_b, coriolis, after, out, ring, outer, second, lap, east_diff, press):
+        return one
+
+    def advance(source, ocean, turn, row, at, cut, emit, northward=None):
+        ahead_press(source, row + 1, at + 1)
+        one = None
+        for f in range(5):
+            ahead(source, row + 1, at + 1, f)
+            one = one or update(source, ocean(), turn(), row, at, cut, emit, northward)
+            one(f)
+
+    def begin(source, rows, ats):
+        for row, at in zip(rows, ats):
+            ahead_press(source, row, at)
+            for f in range(5):
+                ahead(source, row, at, f)
+
+    return begin, advance
+
+
+def swap_halves(value):
+    even = even_half(value.shape[-1])
+    return jnp.where(even, pltpu.roll(value, SUB - 1, 0), pltpu.roll(value, 1, 0))
+
+
+def interior_kernel(
+    planes, cols_a, cols_b, coriolis, after, out, middle, joint, ring, outer, second, centre, sums, east_diff, press
+):
     del after
     half_rows, width = planes.shape[1] - 2 * PAD, planes.shape[3]
+    last = half_rows - 1
     wide = width + LANES
     lon_even = lax.axis_index("lon") % 2 == 0
     get = halo_columns(cols_a, cols_b, lon_even)
@@ -252,7 +280,8 @@
                 outer[f, row + PAD + half_rows] = pltpu.roll(value, SUB - 1, 0)
             if row >= half_rows - HALO:
                 outer[f, row + PAD - half_rows] = pltpu.roll(value, 1, 0)
-    ahead, update = make_step(wide, lap, east_diff, press)
+    begin, advance = make_step(wide, sums, east_diff, press)
+    even = even_half(wide)
 
     def whole(f, row):
         return jnp.concatenate([planes[f, row + PAD], outer[f, row + PAD]], axis=1)
@@ -267,29 +296,56 @@
         out[f, row] = value
 
     def sweep(source, low, high, cut, emit):
-        ahead(source, low - 1)
-        ahead(source, low)
+        begin(source, (low - 1, low), (low - 1 + PAD, low + PAD))
 
         def iteration(row, carry):
-            ahead(source, row + 1)
-            ocean = whole(5, row)[:, :cut]
-            update(source, ocean, coriolis[row + PAD], row, cut, emit)
+            ocean = lambda: whole(5, row)[:, :cut]
+            turn = lambda: coriolis[row + PAD]
+            advance(source, ocean, turn, row, row + PAD, cut, emit)
             return carry
 
         lax.fori_loop(low, high, iteration, 0, unroll=4)
 
     sweep(whole, 2, half_rows - 2, wide, keep)
-    for f in range(5):
-        for i in range(4):
-            ring[f, i] = second[f, 2 + i + PAD]
-            ring[f, 4 + i] = second[f, half_rows - 6 + i + PAD]
+
+    for i in range(4):
+        for f in range(6):
+            joint[f, i] = jnp.where(even, whole(f, i), whole(f, last - i))
+        for f in range(5):
+            ring[f, i] = jnp.where(even, halfway(f, 2 + i), halfway(f, last - 2 - i))
+
+    def mirrored(f, i):
+        return jnp.where(even, whole(f, last - i), whole(f, i))
+
+    north_odd = jnp.where(even, -1.0, 1.0)
+    ocean_of = lambda i, cut: lambda: mirrored(5, i)[:, :cut]
+    turn_of = lambda i: lambda: jnp.where(even[:, :LANES], coriolis[last - i + PAD], coriolis[i + PAD])
+
+    def keep_centre(f, i, value):
+        centre[f, i + 2] = value
+        centre[f, 1 - i] = swap_halves(value)
+
+    begin(mirrored, (-1, 0), (0, 1))
+    for i in range(2):
+        advance(mirrored, ocean_of(i, wide), turn_of(i), i, i + 1, wide, keep_centre, north_odd)
+
+    def centre_halfway(f, i):
+        return centre[f, i + 2] if i < 2 else jnp.where(even, halfway(f, last - i), halfway(f, i))
+
+    def keep_middle(f, i, value):
+        middle[f, i] = value
+
+    begin(centre_halfway, (-1, 0), (0, 1))
+    for i in range(4):
+        advance(centre_halfway, ocean_of(i, width), turn_of(i), i, i + 1, width, keep_middle, north_odd)
+
     sweep(halfway, HALO, half_rows - HALO, width, write)
 
 
 def edges_kernel(
-    planes, outer, coriolis, done, ring, rows_a, rows_b, vel_out, thick_out, trac_out, strip, second, lap, east_diff, press, sem
+    joint, ring, middle, coriolis, done, rows_a, rows_b, vel_out, thick_out, trac_out, strip, first, second, sums, east_diff, press, sem
 ):
-    half_rows, width = planes.shape[1] - 2 * PAD, planes.shape[3]
+    half_rows, width = done.shape[1], done.shape[3]
     wide = width + LANES
     chunks = width // LANES
     levels = SUB // 2
@@ -316,61 +372,53 @@
             strip[f, PAD + i] = done[f, half_rows - PAD + i]
     lat = lax.axis_index("lat")
     lat_even, southmost = lat % 2 == 0, lat == 0
-    even = even_half(wide)
+    even, even_one = even_half(wide), even_half(LANES)
+    even_out = even_half(width)
     corner_a, corner_b = rows_a[chunks * SLOTS], rows_b[chunks * SLOTS]
 
     def message(ref, corner, slot):
         parts = [ref[chunks * slot + c] for c in range(chunks)]
         return jnp.concatenate([*parts, pltpu.roll(corner, -(8 * slot + HALO) % LANES, 1)], axis=1)
 
-    south, north = {}, {}
     for f in range(6):
         reach = HALO if f < 5 else 2
         for m in range(reach // 2):
-            slot = 2 * f + m
-            a, b = message(rows_a, corner_a, slot), message(rows_b, corner_b, slot)
-            from_south = jnp.where(southmost, 0.0, jnp.where(lat_even, b, a))
-            from_north = jnp.where(lat_even, a, b)
-            south[f, 2 * m - reach] = pltpu.roll(from_south, SUB - 1, 0)
-            south[f, 2 * m - reach + 1] = from_south
-            north[f, half_rows + 2 * m] = pltpu.roll(from_north, 1, 0)
-            north[f, half_rows + 2 * m + 1] = from_north
-
-    def whole(f, row):
-        own = jnp.concatenate([planes[f, row + PAD], outer[f, row + PAD]], axis=1)
-        if row < 0:
-            return jnp.where(even, south[f, row], own)
-        if row >= half_rows:
-            return jnp.where(even, own, north[f, row])
-        return own
-
-    ahead, update = make_step(wide, lap, east_diff, press)
-
-    def halfway(f, row):
-        if 2 <= row < 6:
-            return ring[f, row - 2]
-        if half_rows - 6 <= row < half_rows - 2:
-            return ring[f, row - (half_rows - 6) + 4]
-        return second[f, row + PAD]
-
-    def keep(f, row, value):
-        second[f, row + PAD] = value
-
-    def write(f, row, value):
-        strip[f, row if row < HALO else row - half_rows + 2 * PAD] = value
+            slot, opposite = 2 * f + m, 2 * f + reach // 2 - 1 - m
+            south = [message(ref, corner, slot) for ref, corner in ((rows_a, corner_a), (rows_b, corner_b))]
+            north = [message(ref, corner, opposite) for ref, corner in ((rows_a, corner_a), (rows_b, corner_b))]
+            from_south = jnp.where(southmost, 0.0, jnp.where(lat_even, south[1], south[0]))
+            from_north = jnp.where(lat_even, north[0], north[1])
+            row = 2 * m - reach
+            first[f, row + HALO] = jnp.where(even, pltpu.roll(from_south, SUB - 1, 0), from_north)
+            first[f, row + 1 + HALO] = jnp.where(even, from_south, pltpu.roll(from_north, 1, 0))
+
+    def whole(f, i):
+        return first[f, i + HALO] if i < 0 else joint[f, i]
+
+    def halfway(f, i):
+        return second[f, i + 2] if i < 2 else ring[f, i - 2]
+
+    def keep(f, i, value):
+        second[f, i + 2] = value
+
+    def write(f, i, value):
+        other = middle[f, i]
+        strip[f, i] = jnp.where(even_out, value, other)
+        strip[f, 2 * PAD - 1 - i] = jnp.where(even_out, other, value)
+
+    begin, advance = make_step(wide, sums, east_diff, press)
+    north_even = jnp.where(even, 1.0, -1.0)
 
     def sweep(source, low, high, cut, emit):
-        ahead(source, low - 1)
-        ahead(source, low)
-        for row in range(low, high):
-            ahead(source, row + 1)
-            update(source, whole(5, row)[:, :cut], coriolis[row + PAD], row, cut, emit)
+        begin(source, (low - 1, low), (low + 3, low + 4))
+        for i in range(low, high):
+            ocean = lambda: whole(5, i)[:, :cut]
+            turn = lambda: jnp.where(even_one, coriolis[i + PAD], coriolis[half_rows - 1 - i + PAD])
+            advance(source, ocean, turn, i, i + 4, cut, emit, north_even)
 
     sweep(whole, -2, 2, wide, keep)
     sweep(halfway, 0, HALO, width, write)
     copies += copies_out(strip, 0, 0, PAD)
-    sweep(whole, half_rows - 2, half_rows + 2, wide, keep)
-    sweep(halfway, half_rows - HALO, half_rows, width, write)
     copies += copies_out(strip, PAD, half_rows - PAD, PAD)
     for copy in copies:
         copy.wait()
@@ -454,15 +502,27 @@
     rows_a = lax.ppermute(send_a, axes, lat_pairs(0, lat_count, lon_count))
     rows_b = lax.ppermute(send_b, axes, lat_pairs(1, lat_count, lon_count))
 
-    wide_planes = pltpu.VMEM((5, tall, SUB, wide), F32)
-    work = [wide_planes, wide_planes, wide_planes, pltpu.VMEM((tall, SUB, wide), F32)]
-    done, ring, outer = call(
+    def work(length):
+        tall_planes = pltpu.VMEM((5, length, SUB, wide), F32)
+        return [tall_planes, tall_planes, pltpu.VMEM((length, SUB, wide), F32)]
+
+    done, middle, joint, ring = call(
         interior_kernel,
         "interior",
         [VMEM, VMEM, VMEM, VMEM, ANY],
-        (shapes(5, half_rows, SUB, width), shapes(5, 8, SUB, wide), shapes(6, tall, SUB, LANES)),
-        (VMEM, VMEM, VMEM),
-        work,
+        (
+            shapes(5, half_rows, SUB, width),
+            shapes(5, 4, SUB, width),
+            shapes(6, 4, SUB, wide),
+            shapes(5, 4, SUB, wide),
+        ),
+        (VMEM, VMEM, VMEM, VMEM),
+        [
+            pltpu.VMEM((6, tall, SUB, LANES), F32),
+            pltpu.VMEM((5, tall, SUB, wide), F32),
+            pltpu.VMEM((5, 4, SUB, wide), F32),
+            *work(tall),
+        ],
         10**8,
     )(planes, cols_a, cols_b, coriolis, send_a)
 
@@ -472,9 +532,15 @@
         [VMEM] * 7,
         (shapes(*velocity.shape), shapes(*thickness.shape), shapes(*tracers.shape)),
         (HBM, HBM, HBM),
-        [pltpu.VMEM((5, 2 * PAD, SUB, width), F32), *work, dma],
+        [
+            pltpu.VMEM((5, 2 * PAD, SUB, width), F32),
+            pltpu.VMEM((6, HALO, SUB, wide), F32),
+            pltpu.VMEM((5, 4, SUB, wide), F32),
+            *work(10),
+            dma,
+        ],
         10**8,
-    )(planes, outer, coriolis, done, ring, rows_a, rows_b)
+    )(joint, ring, middle, coriolis, done, rows_a, rows_b)
 
 
 def solution(mesh):

time: 24.1 us -> 23.8 us (0.988)
  Pallas kernels: 16.4 us -> 16.1 us
    pallas_call x1, Pallas kernels: 4 us -> 2.54 us  [body(): call(edges_kernel, 'edges', [VMEM] * 7, (shapes(*velocity.shape), shapes(...]
    pallas_call x1, Pallas kernels: 8.03 us -> 9.17 us  [body(): call(interior_kernel, 'interior', [VMEM, VMEM, VMEM, VMEM, ANY], (shapes(...]
  transfers between devices with their start and end apart: 4 -> 4, of which waited for: 0 -> 0; matrix products, arithmetic and copies ran while one was open for 0% -> 0% of each run, Pallas kernels for 43% -> 49%
where the time goes in v3:
time: 23.8 us; the launch traced here: 23.5 us
  Pallas kernels  16.1 us (68%)
  starting transfers between devices  6.76 us (28%)
  between operations  0.69 us (3%)
    pallas_call x1, Pallas kernels, body(): call(interior_kernel, 'interior', [VMEM, VMEM, VMEM, VMEM, ANY], (shapes(...  9.17 us
    ppermute x1, starting transfers between devices, body(): cols_b = lax.ppermute(send_b, 'lon', lon_pairs(1, lon_count))  3.4 us
    ppermute x1, starting transfers between devices, body(): rows_a = lax.ppermute(send_a, axes, lat_pairs(0, lat_count, lon_count))  2.79 us
    pallas_call x1, Pallas kernels, body(): call(edges_kernel, 'edges', [VMEM] * 7, (shapes(*velocity.shape), shapes(...  2.54 us
    pallas_call x1, Pallas kernels, body(): call(functools.partial(load_kernel, lat_count), 'load_fields', [HBM, HBM,...  2.27 us
    pallas_call x1, Pallas kernels, body(): call(columns_kernel, 'pack_columns', [HBM] * 4, (columns, columns), (VMEM...  1.88 us
    ppermute x1, starting transfers between devices, body(): rows_b = lax.ppermute(send_b, axes, lat_pairs(1, lat_count, lon_count))  0.56 us
  transfers between devices with their start and end apart: 4, of which 0 were waited for; matrix products, arithmetic and copies ran while one was open for 0% of the time, Pallas kernels for 49%

profile of v3, /device:TPU:0, one launch (start us, length us, event | category | flops | bytes accessed | tf_op | source)
XLA Modules:
  0.0 23.5 jit_solution(758754235334718637)
XLA Ops:
  0.6 1.9 %pack_columns.1 = (f32[6,8,128]{2,1,0:T(8,128)S(1)}, f32[6,8,128]{2,1,0:T(8,128)S(1)}) custom-call(f32[2,4,64,512]{3,2,1,0:T(8,128)} %vel.3, f32[4,64,512]{2,1,0:T(8,128)} %thick.3, f32[2,4,64,512]{3,2,1,0:T(8,128)} %trac.3, s32[4,64,512]{2,1,0:T(8,128)} %mask.3), custom_call_target="tpu_custom_call" | custom-call | flops 1000000 | bytes 100000 | tf_op jit(solution)/shard_map/pack_columns/pallas_call | solution.py:469
  2.5 3.4 %collective-permute-start.1 = (f32[6,8,128]{2,1,0:T(8,128)S(1)}, f32[6,8,128]{2,1,0:T(8,128)S(1)}, u32[]{:S(2)}, u32[]{:S(2)}) collective-permute-start(f32[6,8,128]{2,1,0:T(8,128)S(1)} %get-tuple-element.15), channel_id=1, source_target_pairs={{0,28},{4,8},{8,4},{12,16},{16,12},{20,24},{24,20},{28,0},{1,29},{... | collective-permute-start | bytes 73736 | tf_op jit(solution)/shard_map/ppermute | solution.py:479
  5.9 0.0 collective-permute-start
  5.9 2.3 %load_fields.1 = (f32[6,48,8,512]{3,2,1,0:T(8,128)S(1)}, f32[48,8,128]{2,1,0:T(8,128)S(1)}) custom-call(f32[2,4,64,512]{3,2,1,0:T(8,128)} %vel.3, f32[4,64,512]{2,1,0:T(8,128)} %thick.3, f32[2,4,64,512]{3,2,1,0:T(8,128)} %trac.3, s32[4,64,512]{2,1,0:T(8,128)} %mask.3, f32[6,8,128]{2,1,0:T(8,128)S(1)} %get-tuple-element.13.after), custom_call_target="tpu_custom_call" | custom-call | flops 100000000 | bytes 10000000 | tf_op jit(solution)/shard_map/load_fields/pallas_call | solution.py:481
  8.2 0.0 collective-permute-done.1.cols_b
  8.2 0.0 collective-permute-done.cols_a
  8.2 0.2 pack_rows.1
  8.5 0.6 %collective-permute-start.3 = (f32[45,8,128]{2,1,0:T(8,128)S(1)}, f32[45,8,128]{2,1,0:T(8,128)S(1)}, u32[]{:S(2)}, u32[]{:S(2)}) collective-permute-start(f32[45,8,128]{2,1,0:T(8,128)S(1)} %get-tuple-element.22), channel_id=1, source_target_pairs={{0,4},{4,0},{8,12},{12,8},{16,20},{20,16},{24,28},{28,24},{1,2},{5... | collective-permute-start | bytes 552968 | tf_op jit(solution)/shard_map/ppermute | solution.py:503
  9.0 2.8 %collective-permute-start.2 = (f32[45,8,128]{2,1,0:T(8,128)S(1)}, f32[45,8,128]{2,1,0:T(8,128)S(1)}, u32[]{:S(2)}, u32[]{:S(2)}) collective-permute-start(f32[45,8,128]{2,1,0:T(8,128)S(1)} %get-tuple-element.17.after), channel_id=1, source_target_pairs={{0,1},{4,5},{8,9},{12,13},{16,17},{20,21},{24,25},{28,29},{1,0},{5... | collective-permute-start | bytes 552968 | tf_op jit(solution)/shard_map/ppermute | solution.py:502
  11.8 9.2 %interior.1 = (f32[5,32,8,512]{3,2,1,0:T(8,128)S(1)}, f32[5,4,8,512]{3,2,1,0:T(8,128)S(1)}, f32[6,4,8,640]{3,2,1,0:T(8,128)S(1)}, f32[5,4,8,640]{3,2,1,0:T(8,128)S(1)}) custom-call(f32[6,48,8,512]{3,2,1,0:T(8,128)S(1)} %get-tuple-element.14.planes, f32[6,8,128]{2,1,0:T(8,128)S(1)} %collective-permute-done.cols_a, ...), custom_call_target="tpu_custom_call" | custom-call | flops 100000000 | bytes 10000000 | tf_op jit(solution)/shard_map/interior/pallas_call | solution.py:509
  21.0 0.0 collective-permute-done.3.rows_b
  21.0 0.0 collective-permute-done.2.rows_a
  21.0 2.5 %edges.1 = (f32[2,4,64,512]{3,2,1,0:T(8,128)}, f32[4,64,512]{2,1,0:T(8,128)}, f32[2,4,64,512]{3,2,1,0:T(8,128)}) custom-call(f32[6,4,8,640]{3,2,1,0:T(8,128)S(1)} %get-tuple-element.18.joint, f32[5,4,8,640]{3,2,1,0:T(8,128)S(1)} %get-tuple-element.19.ring, f32[5,4,8,512]{3,2,1,0:T(8,128)S(1)} %get-tuple-element.20.middle, ...), custom_call_target="tpu_custom_call" | custom-call | flops 100000000 | bytes 10000000 | tf_op jit(solution)/shard_map/edges/pallas_call | solution.py:529
Async XLA Ops:
  2.5 5.7 %collective-permute-start.1 = (f32[6,8,128]{2,1,0:T(8,128)S(1)}, f32[6,8,128]{2,1,0:T(8,128)S(1)}, u32[]{:S(2)}, u32[]{:S(2)}) collective-permute-start(f32[6,8,128]{2,1,0:T(8,128)S(1)} %get-tuple-element.15), channel_id=1, source_target_pairs={{0,28},{4,8},{8,4},{12,16},{16,12},{20,24},{24,20},{28,0},{1,29},{... | collective-permute-start | bytes 73736 | tf_op jit(solution)/shard_map/ppermute | solution.py:479
  5.9 2.3 %collective-permute-start = (f32[6,8,128]{2,1,0:T(8,128)S(1)}, f32[6,8,128]{2,1,0:T(8,128)S(1)}, u32[]{:S(2)}, u32[]{:S(2)}) collective-permute-start(f32[6,8,128]{2,1,0:T(8,128)S(1)} %get-tuple-element.13.after), channel_id=1, source_target_pairs={{0,4},{4,0},{8,12},{12,8},{16,20},{20,16},{24,28},{28,24},{1,5},{5... | collective-permute-start | bytes 73736 | tf_op jit(solution)/shard_map/ppermute | solution.py:478
  8.5 12.5 %collective-permute-start.3 = (f32[45,8,128]{2,1,0:T(8,128)S(1)}, f32[45,8,128]{2,1,0:T(8,128)S(1)}, u32[]{:S(2)}, u32[]{:S(2)}) collective-permute-start(f32[45,8,128]{2,1,0:T(8,128)S(1)} %get-tuple-element.22), channel_id=1, source_target_pairs={{0,4},{4,0},{8,12},{12,8},{16,20},{20,16},{24,28},{28,24},{1,2},{5... | collective-permute-start | bytes 552968 | tf_op jit(solution)/shard_map/ppermute | solution.py:503
  9.0 12.0 %collective-permute-start.2 = (f32[45,8,128]{2,1,0:T(8,128)S(1)}, f32[45,8,128]{2,1,0:T(8,128)S(1)}, u32[]{:S(2)}, u32[]{:S(2)}) collective-permute-start(f32[45,8,128]{2,1,0:T(8,128)S(1)} %get-tuple-element.17.after), channel_id=1, source_target_pairs={{0,1},{4,5},{8,9},{12,13},{16,17},{20,21},{24,25},{28,29},{1,0},{5... | collective-permute-start | bytes 552968 | tf_op jit(solution)/shard_map/ppermute | solution.py:502

commit v4 on v3

--- a/solution.py
+++ b/solution.py
@@ -19,6 +19,7 @@
 LANES = 128
 SUB = 8
 SLOTS = 11
+ROLLED = 4
 F32 = jnp.float32
 VMEM = pl.BlockSpec(memory_space=pltpu.VMEM)
 HBM = pl.BlockSpec(memory_space=pltpu.HBM)
@@ -36,34 +37,31 @@
     return jnp.concatenate(parts, axis=1)
 
 
-def run_copies(copies):
-    for copy in copies:
-        copy.start()
-    for copy in copies:
-        copy.wait()
-
-
 def columns_kernel(vel, thick, trac, mask, out_a, out_b, edges, land, sem):
     levels, rows, width = thick.shape
     half_rows = rows // 2
-    copies = []
+    groups = {0: [], 2: [], 3: [], 5: []}
     for side in range(2):
         lanes = pl.ds(side * (width - LANES), LANES)
         to = pl.ds(side * LANES, LANES)
         for level in range(levels):
             for half in range(2):
                 at, s = pl.ds(half * half_rows, half_rows), 2 * level + half
-                for source, target in (
-                    (vel.at[:, level, at, lanes], edges.at[0:2, :, s, to]),
-                    (thick.at[level, at, lanes], edges.at[2, :, s, to]),
-                    (trac.at[:, level, at, lanes], edges.at[3:5, :, s, to]),
-                    (mask.at[level, at, lanes], land.at[:, s, to]),
+                for f, source, target in (
+                    (0, vel.at[:, level, at, lanes], edges.at[0:2, :, s, to]),
+                    (2, thick.at[level, at, lanes], edges.at[2, :, s, to]),
+                    (3, trac.at[:, level, at, lanes], edges.at[3:5, :, s, to]),
+                    (5, mask.at[level, at, lanes], land.at[:, s, to]),
                 ):
-                    copies.append(pltpu.make_async_copy(source, target, sem))
-    run_copies(copies)
+                    groups[f].append(pltpu.make_async_copy(source, target, sem.at[f]))
+    for f in groups:
+        for copy in groups[f]:
+            copy.start()
     lon_even = lax.axis_index("lon") % 2 == 0
     group = lax.broadcasted_iota(jnp.int32, (SUB, LANES), 1) // HALO
     for f in range(6):
+        for copy in groups.get(f, ()):
+            copy.wait()
         west = east = jnp.zeros((SUB, LANES), F32)
         for row in range(half_rows):
             pair = edges[f, row] if f < 5 else HYPERVISCOSITY * land[row].astype(F32)
@@ -74,25 +72,26 @@
         out_b[f] = jnp.where(lon_even, west, east)
 
 
-def load_kernel(lat_count, vel, thick, trac, mask, after, planes, coriolis, land, sem):
+def load_kernel(lat_count, vel, thick, trac, mask, after, planes, from_east, from_west, coriolis, land, sem):
     del after
     levels, rows, width = thick.shape
     half_rows = rows // 2
     length = half_rows + PAD
-    copies = []
+    groups = {0: [], 2: [], 3: [], 5: []}
     for level in range(levels):
         for half in range(2):
             at, s = pl.ds(half * (half_rows - PAD), length), 2 * level + half
             to = pl.ds((1 - half) * PAD, length)
-            for source, target in (
-                (vel.at[:, level, at, :], planes.at[0:2, to, s, :]),
-                (thick.at[level, at, :], planes.at[2, to, s, :]),
-                (trac.at[:, level, at, :], planes.at[3:5, to, s, :]),
-                (mask.at[level, at, :], land.at[to, s, :]),
+            for f, source, target in (
+                (0, vel.at[:, level, at, :], planes.at[0:2, to, s, :]),
+                (2, thick.at[level, at, :], planes.at[2, to, s, :]),
+                (3, trac.at[:, level, at, :], planes.at[3:5, to, s, :]),
+                (5, mask.at[level, at, :], land.at[to, s, :]),
             ):
-                copies.append(pltpu.make_async_copy(source, target, sem))
-    for copy in copies:
-        copy.start()
+                groups[f].append(pltpu.make_async_copy(source, target, sem.at[f]))
+    for f in groups:
+        for copy in groups[f]:
+            copy.start()
     total = rows * lat_count
     half = lax.broadcasted_iota(jnp.int32, (SUB, LANES), 0) % 2
     first = lax.axis_index("lat") * rows + half * half_rows
@@ -101,28 +100,36 @@
         folded = jnp.where(ids >= total, 2 * total - 1 - ids, ids)
         angle = jnp.pi * (folded.astype(F32) + 0.5) / total - jnp.pi / 2
         coriolis[row + PAD] = (CORIOLIS / HYPERVISCOSITY) * jnp.sin(angle)
-    for copy in copies:
-        copy.wait()
+    for f in range(6):
+        for copy in groups.get(f, ()):
+            copy.wait()
+        if f == 5:
+            break
+        for row in range(PAD, half_rows + PAD) if f < ROLLED else ():
+            value = planes[f, row]
+            from_east[f, row] = pltpu.roll(value, width - 1, 1)
+            from_west[f, row] = pltpu.roll(value, 1, 1)
     for row in range(PAD - 2, half_rows + PAD + 2):
         planes[5, row] = HYPERVISCOSITY * land[row].astype(F32)
 
 
 def halo_columns(cols_a, cols_b, lon_even):
-    lane = lax.broadcasted_iota(jnp.int32, (SUB, LANES), 1)
-
     def get(f):
         a, b = cols_a[f], cols_b[f]
-        from_west = jnp.where(lon_even, b, a)
-        from_east = jnp.where(lon_even, a, b)
-
-        def row(r):
-            east = pltpu.roll(from_east, -HALO * r % LANES, 1)
-            west = pltpu.roll(from_west, -HALO * (r + 1) % LANES, 1)
-            return jnp.where(lane < LANES // 2, east, west)
-
-        return row
+        return halo_of(jnp.where(lon_even, a, b), jnp.where(lon_even, b, a))
 
     return get
+
+
+def halo_of(from_east, from_west):
+    lane = lax.broadcasted_iota(jnp.int32, (SUB, LANES), 1)
+
+    def row(r):
+        east = pltpu.roll(from_east, (LANES - HALO * r) % LANES, 1)
+        west = pltpu.roll(from_west, LANES - HALO * (r + 1), 1)
+        return jnp.where(lane < LANES // 2, east, west)
+
+    return row
 
 
 def rows_kernel(lat_count, planes, cols_a, cols_b, out_a, out_b):
@@ -194,17 +201,21 @@
     def shifts(value):
         return pltpu.roll(value, wide - 1, 1), pltpu.roll(value, 1, 1)
 
-    def ahead(source, row, at, f):
-        to_east, to_west = shifts(source(f, row))
+    def ahead(source, row, at, f, shifted):
+        to_east, to_west = shifted(f, row) if shifted else shifts(source(f, row))
         sums[f, at] = (to_east + to_west) + (source(f, row + 1) + source(f, row - 1))
         east_diff[f, at] = to_east - to_west
 
+    def weighed_down(thick, temp, salt):
+        lanes = slice(0, thick.shape[-1])
+        part = weight[:, lanes] * thick + ((0.08 * slope) * salt - (0.1 * slope) * temp)
+        part = part + jnp.where(below_one[:, lanes], pltpu.roll(part, 2, 0), 0.0)
+        return part + jnp.where(below_two[:, lanes], pltpu.roll(part, 4, 0), 0.0)
+
     def ahead_press(source, row, at):
-        part = weight * source(2, row) + ((0.08 * slope) * source(4, row) - (0.1 * slope) * source(3, row))
-        part = part + jnp.where(below_one, pltpu.roll(part, 2, 0), 0.0)
-        press[at] = part + jnp.where(below_two, pltpu.roll(part, 4, 0), 0.0)
-
-    def update(source, ocean, turn, row, at, cut, emit, northward):
+        press[at] = weighed_down(source(2, row), source(3, row), source(4, row))
+
+    def update_row(source, ocean, turn, row, at, cut, emit, northward=None, roll_press=False):
         lanes = slice(0, cut)
         turn = jnp.concatenate([turn] * (cut // LANES), axis=1)
         u, v = source(0, row)[:, lanes], source(1, row)[:, lanes]
@@ -214,8 +225,11 @@
 
         def add_on(f):
             if f == 0:
-                p_east, p_west = shifts(press[at])
-                return turn * v + (p_east - p_west)[:, lanes]
+                if roll_press:
+                    p_east, p_west = shifts(press[at])
+                    return turn * v + (p_east - p_west)[:, lanes]
+                slopes = [east_diff[field, at, :, lanes] for field in (2, 3, 4)]
+                return turn * v + weighed_down(*slopes)
             if f == 1:
                 rise = press[at + 1, :, lanes] - press[at - 1, :, lanes]
                 if northward is not None:
@@ -238,23 +252,15 @@
                 value = value + add_on(f)
             emit(f, row, value * ocean)
 
-        return one
-
-    def advance(source, ocean, turn, row, at, cut, emit, northward=None):
-        ahead_press(source, row + 1, at + 1)
-        one = None
         for f in range(5):
-            ahead(source, row + 1, at + 1, f)
-            one = one or update(source, ocean(), turn(), row, at, cut, emit, northward)
             one(f)
 
-    def begin(source, rows, ats):
-        for row, at in zip(rows, ats):
-            ahead_press(source, row, at)
-            for f in range(5):
-                ahead(source, row, at, f)
-
-    return begin, advance
+    def ahead_row(source, row, at, shifted=None):
+        ahead_press(source, row, at)
+        for f in range(5):
+            ahead(source, row, at, f, shifted)
+
+    return ahead_row, update_row
 
 
 def swap_halves(value):
@@ -263,29 +269,63 @@
 
 
 def interior_kernel(
-    planes, cols_a, cols_b, coriolis, after, out, middle, joint, ring, outer, second, centre, sums, east_diff, press
+    planes,
+    from_east,
+    from_west,
+    cols_a,
+    cols_b,
+    coriolis,
+    after,
+    out,
+    middle,
+    joint,
+    ring,
+    joint_sums,
+    joint_diff,
+    joint_press,
+    outer,
+    sides,
+    second,
+    centre,
+    sums,
+    east_diff,
+    press,
 ):
     del after
     half_rows, width = planes.shape[1] - 2 * PAD, planes.shape[3]
     last = half_rows - 1
     wide = width + LANES
     lon_even = lax.axis_index("lon") % 2 == 0
-    get = halo_columns(cols_a, cols_b, lon_even)
     for f in range(6):
-        column = get(f)
-        for row in range(half_rows):
-            value = column(row)
-            outer[f, row + PAD] = value
-            if row < HALO:
-                outer[f, row + PAD + half_rows] = pltpu.roll(value, SUB - 1, 0)
-            if row >= half_rows - HALO:
-                outer[f, row + PAD - half_rows] = pltpu.roll(value, 1, 0)
-    begin, advance = make_step(wide, sums, east_diff, press)
+        a, b = cols_a[f], cols_b[f]
+        sides[0, f] = jnp.where(lon_even, a, b)
+        sides[1, f] = jnp.where(lon_even, b, a)
+
+    def add_halo(row):
+        for f in range(6):
+            outer[f, row + PAD] = halo_of(sides[0, f], sides[1, f])(row)
+
+    for row in range(4):
+        add_halo(row)
+    ahead_row, update_row = make_step(wide, sums, east_diff, press)
     even = even_half(wide)
+    lane = lax.broadcasted_iota(jnp.int32, (SUB, LANES), 1)
+    at_first, at_last = lane == 0, lane == LANES - 1
 
     def whole(f, row):
         return jnp.concatenate([planes[f, row + PAD], outer[f, row + PAD]], axis=1)
 
+    def whole_shifted(f, row):
+        at = row + PAD
+        if f >= ROLLED:
+            return pltpu.roll(whole(f, row), wide - 1, 1), pltpu.roll(whole(f, row), 1, 1)
+        east, west, halo = from_east[f, at], from_west[f, at], outer[f, at]
+        halo_east, halo_west = pltpu.roll(halo, LANES - 1, 1), pltpu.roll(halo, 1, 1)
+        tail, head = east[:, width - LANES :], west[:, :LANES]
+        east = [east[:, : width - LANES], jnp.where(at_last, halo_east, tail), jnp.where(at_last, tail, halo_east)]
+        west = [jnp.where(at_first, halo_west, head), west[:, LANES:], jnp.where(at_first, head, halo_west)]
+        return jnp.concatenate(east, axis=1), jnp.concatenate(west, axis=1)
+
     def keep(f, row, value):
         second[f, row + PAD] = value
 
@@ -295,55 +335,119 @@
     def write(f, row, value):
         out[f, row] = value
 
-    def sweep(source, low, high, cut, emit):
-        begin(source, (low - 1, low), (low - 1 + PAD, low + PAD))
+    def sweep(source, low, high, cut, emit, shifted=None):
+        ahead_row(source, low - 1, low - 1 + PAD, shifted)
+        ahead_row(source, low, low + PAD, shifted)
 
         def iteration(row, carry):
-            ocean = lambda: whole(5, row)[:, :cut]
-            turn = lambda: coriolis[row + PAD]
-            advance(source, ocean, turn, row, row + PAD, cut, emit)
+            if shifted:
+                add_halo(row + 2)
+            ahead_row(source, row + 1, row + 1 + PAD, shifted)
+            ocean, turn = whole(5, row)[:, :cut], coriolis[row + PAD]
+            update_row(source, ocean, turn, row, row + PAD, cut, emit, roll_press=bool(shifted))
             return carry
 
-        lax.fori_loop(low, high, iteration, 0, unroll=4)
-
-    sweep(whole, 2, half_rows - 2, wide, keep)
-
+        lax.fori_loop(low, high, iteration, 0, unroll=(high - low) // 2)
+
+    def outer_pair(ref, i):
+        return jnp.where(even, ref[i + PAD], ref[last - i + PAD])
+
+    def inner_pair(ref, i):
+        return jnp.where(even, ref[last - i + PAD], ref[i + PAD])
+
+    def save_outer(step, i):
+        for f in range(5):
+            for k in range(2):
+                joint_sums[step, f, k] = outer_pair(sums.at[f], i + k)
+            joint_diff[step, f] = outer_pair(east_diff.at[f], i)
+        for k in range(2):
+            joint_press[step, k] = outer_pair(press, i + k)
+
+    def take_inner(i):
+        for f in range(5):
+            sums[f, i + 1] = inner_pair(sums.at[f], i)
+            east_diff[f, i + 1] = inner_pair(east_diff.at[f], i)
+        press[i + 1] = inner_pair(press, i)
+
+    def fold_inner():
+        for f in range(5):
+            sums[f, 0] = swap_halves(sums[f, 1])
+        press[0] = swap_halves(press[1])
+
+    sweep(whole, 2, half_rows - 2, wide, keep, whole_shifted)
+    for f in range(5):
+        outer[f, half_rows + PAD] = pltpu.roll(outer[f, PAD], SUB - 1, 0)
+        outer[f, PAD - 1] = pltpu.roll(outer[f, last + PAD], 1, 0)
+    save_outer(0, 1)
     for i in range(4):
         for f in range(6):
             joint[f, i] = jnp.where(even, whole(f, i), whole(f, last - i))
         for f in range(5):
-            ring[f, i] = jnp.where(even, halfway(f, 2 + i), halfway(f, last - 2 - i))
+            ring[f, i] = outer_pair(second.at[f], 2 + i)
 
     def mirrored(f, i):
         return jnp.where(even, whole(f, last - i), whole(f, i))
 
+    def mirrored_shifted(f, i):
+        south, north = whole_shifted(f, last - i), whole_shifted(f, i)
+        return [jnp.where(even, one, other) for one, other in zip(south, north)]
+
     north_odd = jnp.where(even, -1.0, 1.0)
-    ocean_of = lambda i, cut: lambda: mirrored(5, i)[:, :cut]
-    turn_of = lambda i: lambda: jnp.where(even[:, :LANES], coriolis[last - i + PAD], coriolis[i + PAD])
+
+    def turn_of(i):
+        return jnp.where(even[:, :LANES], coriolis[last - i + PAD], coriolis[i + PAD])
 
     def keep_centre(f, i, value):
         centre[f, i + 2] = value
         centre[f, 1 - i] = swap_halves(value)
 
-    begin(mirrored, (-1, 0), (0, 1))
+    ahead_row(mirrored, 0, 1, mirrored_shifted)
+    fold_inner()
+    take_inner(1)
+    take_inner(2)
     for i in range(2):
-        advance(mirrored, ocean_of(i, wide), turn_of(i), i, i + 1, wide, keep_centre, north_odd)
+        update_row(mirrored, mirrored(5, i), turn_of(i), i, i + 1, wide, keep_centre, north_odd)
+
+    sweep(halfway, HALO, half_rows - HALO, width, write)
+    save_outer(1, 3)
 
     def centre_halfway(f, i):
-        return centre[f, i + 2] if i < 2 else jnp.where(even, halfway(f, last - i), halfway(f, i))
+        return centre[f, i + 2] if i < 2 else inner_pair(second.at[f], i)
 
     def keep_middle(f, i, value):
         middle[f, i] = value
 
-    begin(centre_halfway, (-1, 0), (0, 1))
+    for i in range(3):
+        ahead_row(centre_halfway, i, i + 1)
+    fold_inner()
+    take_inner(3)
+    take_inner(4)
     for i in range(4):
-        advance(centre_halfway, ocean_of(i, width), turn_of(i), i, i + 1, width, keep_middle, north_odd)
-
-    sweep(halfway, HALO, half_rows - HALO, width, write)
+        ocean = mirrored(5, i)[:, :width]
+        update_row(centre_halfway, ocean, turn_of(i), i, i + 1, width, keep_middle, north_odd)
 
 
 def edges_kernel(
-    joint, ring, middle, coriolis, done, rows_a, rows_b, vel_out, thick_out, trac_out, strip, first, second, sums, east_diff, press, sem
+    joint,
+    ring,
+    joint_sums,
+    joint_diff,
+    joint_press,
+    middle,
+    coriolis,
+    done,
+    rows_a,
+    rows_b,
+    vel_out,
+    thick_out,
+    trac_out,
+    strip,
+    first,
+    second,
+    sums,
+    east_diff,
+    press,
+    sem,
 ):
     half_rows, width = done.shape[1], done.shape[3]
     wide = width + LANES
@@ -406,18 +510,27 @@
         strip[f, i] = jnp.where(even_out, value, other)
         strip[f, 2 * PAD - 1 - i] = jnp.where(even_out, other, value)
 
-    begin, advance = make_step(wide, sums, east_diff, press)
+    ahead_row, update_row = make_step(wide, sums, east_diff, press)
     north_even = jnp.where(even, 1.0, -1.0)
 
-    def sweep(source, low, high, cut, emit):
-        begin(source, (low - 1, low), (low + 3, low + 4))
+    def sweep(source, step, low, cut, emit):
+        high = low + 4
+        for k in range(2):
+            for f in range(5):
+                sums[f, high - 1 + k + 4] = joint_sums[step, f, k]
+            press[high - 1 + k + 4] = joint_press[step, k]
+        for f in range(5):
+            east_diff[f, high - 1 + 4] = joint_diff[step, f]
+        ahead_row(source, low - 1, low + 3)
+        ahead_row(source, low, low + 4)
         for i in range(low, high):
-            ocean = lambda: whole(5, i)[:, :cut]
-            turn = lambda: jnp.where(even_one, coriolis[i + PAD], coriolis[half_rows - 1 - i + PAD])
-            advance(source, ocean, turn, i, i + 4, cut, emit, north_even)
-
-    sweep(whole, -2, 2, wide, keep)
-    sweep(halfway, 0, HALO, width, write)
+            if i + 1 < high - 1:
+                ahead_row(source, i + 1, i + 5)
+            turn = jnp.where(even_one, coriolis[i + PAD], coriolis[half_rows - 1 - i + PAD])
+            update_row(source, whole(5, i)[:, :cut], turn, i, i + 4, cut, emit, north_even)
+
+    sweep(whole, 0, -2, wide, keep)
+    sweep(halfway, 1, 0, width, write)
     copies += copies_out(strip, 0, 0, PAD)
     copies += copies_out(strip, PAD, half_rows - PAD, PAD)
     for copy in copies:
@@ -460,7 +573,7 @@
             in_specs=in_specs,
             out_specs=out_specs,
             scratch_shapes=scratch,
-            compiler_params=pltpu.CompilerParams(vmem_limit_bytes=40 * 2**20),
+            compiler_params=pltpu.CompilerParams(vmem_limit_bytes=24 * 2**20),
             cost_estimate=pl.CostEstimate(flops=flops, bytes_accessed=flops // 10, transcendentals=0),
             name=name,
         )
@@ -472,19 +585,20 @@
         [HBM] * 4,
         (columns, columns),
         (VMEM, VMEM),
-        [pltpu.VMEM((5, half_rows, SUB, 2 * LANES), F32), pltpu.VMEM((half_rows, SUB, 2 * LANES), jnp.int32), dma],
+        [pltpu.VMEM((5, half_rows, SUB, 2 * LANES), F32), pltpu.VMEM((half_rows, SUB, 2 * LANES), jnp.int32), dma((6,))],
         10**6,
     )(*fields)
     cols_a = lax.ppermute(send_a, "lon", lon_pairs(0, lon_count))
     cols_b = lax.ppermute(send_b, "lon", lon_pairs(1, lon_count))
 
-    planes, coriolis = call(
+    block = shapes(ROLLED, tall, SUB, width)
+    planes, from_east, from_west, coriolis = call(
         functools.partial(load_kernel, lat_count),
         "load_fields",
         [HBM, HBM, HBM, HBM, ANY],
-        (shapes(6, tall, SUB, width), shapes(tall, SUB, LANES)),
-        (VMEM, VMEM),
-        [pltpu.VMEM((tall, SUB, width), jnp.int32), dma],
+        (shapes(6, tall, SUB, width), block, block, shapes(tall, SUB, LANES)),
+        (VMEM,) * 4,
+        [pltpu.VMEM((tall, SUB, width), jnp.int32), dma((6,))],
         10**8,
     )(*fields, send_a)
 
@@ -506,30 +620,34 @@
         tall_planes = pltpu.VMEM((5, length, SUB, wide), F32)
         return [tall_planes, tall_planes, pltpu.VMEM((length, SUB, wide), F32)]
 
-    done, middle, joint, ring = call(
+    done, middle, *kept = call(
         interior_kernel,
         "interior",
-        [VMEM, VMEM, VMEM, VMEM, ANY],
+        [VMEM] * 6 + [ANY],
         (
             shapes(5, half_rows, SUB, width),
             shapes(5, 4, SUB, width),
             shapes(6, 4, SUB, wide),
             shapes(5, 4, SUB, wide),
+            shapes(2, 5, 2, SUB, wide),
+            shapes(2, 5, SUB, wide),
+            shapes(2, 2, SUB, wide),
         ),
-        (VMEM, VMEM, VMEM, VMEM),
+        (VMEM,) * 7,
         [
             pltpu.VMEM((6, tall, SUB, LANES), F32),
+            pltpu.VMEM((2, 6, SUB, LANES), F32),
             pltpu.VMEM((5, tall, SUB, wide), F32),
             pltpu.VMEM((5, 4, SUB, wide), F32),
             *work(tall),
         ],
         10**8,
-    )(planes, cols_a, cols_b, coriolis, send_a)
+    )(planes, from_east, from_west, cols_a, cols_b, coriolis, send_a)
 
     return call(
         edges_kernel,
         "edges",
-        [VMEM] * 7,
+        [VMEM] * 10,
         (shapes(*velocity.shape), shapes(*thickness.shape), shapes(*tracers.shape)),
         (HBM, HBM, HBM),
         [
@@ -540,7 +658,7 @@
             dma,
         ],
         10**8,
-    )(joint, ring, middle, coriolis, done, rows_a, rows_b)
+    )(*kept, middle, coriolis, done, rows_a, rows_b)
 
 
 def solution(mesh):

time: 23.8 us -> 22.2 us (0.933)
  Pallas kernels: 16.1 us -> 14.6 us
    pallas_call x2, Pallas kernels: 11.7 us -> 9.89 us  [the longest x1 7.54 us: body(): call(interior_kernel, 'interior', [VMEM] * 6 + [ANY], (shapes(5, half_row...]
    pallas_call x1, Pallas kernels: 2.27 us -> 2.78 us  [body(): call(functools.partial(load_kernel, lat_count), 'load_fields', [HBM, HBM,...]
  transfers between devices with their start and end apart: 4 -> 4, of which waited for: 0 -> 0; matrix products, arithmetic and copies ran while one was open for 0% -> 0% of each run, Pallas kernels for 49% -> 47%
where the time goes in v4:
time: 22.2 us; the launch traced here: 22 us
  Pallas kernels  14.6 us (66%)
  starting transfers between devices  6.62 us (30%)
  between operations  0.69 us (3%)
    pallas_call x1, Pallas kernels, body(): call(interior_kernel, 'interior', [VMEM] * 6 + [ANY], (shapes(5, half_row...  7.54 us
    ppermute x1, starting transfers between devices, body(): cols_b = lax.ppermute(send_b, 'lon', lon_pairs(1, lon_count))  3.4 us
    pallas_call x1, Pallas kernels, body(): call(functools.partial(load_kernel, lat_count), 'load_fields', [HBM, HBM,...  2.78 us
    ppermute x1, starting transfers between devices, body(): rows_a = lax.ppermute(send_a, axes, lat_pairs(0, lat_count, lon_count))  2.65 us
    pallas_call x1, Pallas kernels, body(): call(edges_kernel, 'edges', [VMEM] * 10, (shapes(*velocity.shape), shapes...  2.34 us
    pallas_call x1, Pallas kernels, body(): call(columns_kernel, 'pack_columns', [HBM] * 4, (columns, columns), (VMEM...  1.74 us
    ppermute x1, starting transfers between devices, body(): rows_b = lax.ppermute(send_b, axes, lat_pairs(1, lat_count, lon_count))  0.57 us
  transfers between devices with their start and end apart: 4, of which 0 were waited for; matrix products, arithmetic and copies ran while one was open for 0% of the time, Pallas kernels for 47%

profile of v4, /device:TPU:0, one launch (start us, length us, event | category | flops | bytes accessed | tf_op | source)
XLA Modules:
  0.0 22.0 jit_solution(12692060232952626410)
XLA Ops:
  0.6 1.7 %pack_columns.1 = (f32[6,8,128]{2,1,0:T(8,128)S(1)}, f32[6,8,128]{2,1,0:T(8,128)S(1)}) custom-call(f32[2,4,64,512]{3,2,1,0:T(8,128)} %vel.3, f32[4,64,512]{2,1,0:T(8,128)} %thick.3, f32[2,4,64,512]{3,2,1,0:T(8,128)} %trac.3, s32[4,64,512]{2,1,0:T(8,128)} %mask.3), custom_call_target="tpu_custom_call" | custom-call | flops 1000000 | bytes 100000 | tf_op jit(solution)/shard_map/pack_columns/pallas_call | solution.py:582
  2.4 3.4 %collective-permute-start.1 = (f32[6,8,128]{2,1,0:T(8,128)S(1)}, f32[6,8,128]{2,1,0:T(8,128)S(1)}, u32[]{:S(2)}, u32[]{:S(2)}) collective-permute-start(f32[6,8,128]{2,1,0:T(8,128)S(1)} %get-tuple-element.22), channel_id=1, source_target_pairs={{0,28},{4,8},{8,4},{12,16},{16,12},{20,24},{24,20},{28,0},{1,29},{... | collective-permute-start | bytes 73736 | tf_op jit(solution)/shard_map/ppermute | solution.py:592
  5.8 0.0 collective-permute-start
  5.8 2.8 %load_fields.1 = (f32[6,48,8,512]{3,2,1,0:T(8,128)S(1)}, f32[4,48,8,512]{3,2,1,0:T(8,128)S(1)}, f32[4,48,8,512]{3,2,1,0:T(8,128)S(1)}, f32[48,8,128]{2,1,0:T(8,128)S(1)}) custom-call(f32[2,4,64,512]{3,2,1,0:T(8,128)} %vel.3, f32[4,64,512]{2,1,0:T(8,128)} %thick.3, f32[2,4,64,512]{3,2,1,0:T(8,128)} %trac.3, s32[4,64,512]{2,1,0:T(8,128)} %mask.3, ...), custom_call_target="tpu_custom_call" | custom-call | flops 100000000 | bytes 10000000 | tf_op jit(solution)/shard_map/load_fields/pallas_call | solution.py:595
  8.6 0.0 collective-permute-done.1.cols_b
  8.6 0.0 collective-permute-done.cols_a
  8.6 0.2 %pack_rows.1 = (f32[45,8,128]{2,1,0:T(8,128)S(1)}, f32[45,8,128]{2,1,0:T(8,128)S(1)}) custom-call(f32[6,48,8,512]{3,2,1,0:T(8,128)S(1)} %get-tuple-element.19.planes, f32[6,8,128]{2,1,0:T(8,128)S(1)} %collective-permute-done.cols_a, f32[6,8,128]{2,1,0:T(8,128)S(1)} %collective-permute-done.1.cols_b), custom_call_target="tpu_custom_call" | custom-call | flops 1000000 | bytes 100000 | tf_op jit(solution)/shard_map/pack_rows/pallas_call | solution.py:606
  8.8 0.6 %collective-permute-start.3 = (f32[45,8,128]{2,1,0:T(8,128)S(1)}, f32[45,8,128]{2,1,0:T(8,128)S(1)}, u32[]{:S(2)}, u32[]{:S(2)}) collective-permute-start(f32[45,8,128]{2,1,0:T(8,128)S(1)} %get-tuple-element.32), channel_id=1, source_target_pairs={{0,4},{4,0},{8,12},{12,8},{16,20},{20,16},{24,28},{28,24},{1,2},{5... | collective-permute-start | bytes 552968 | tf_op jit(solution)/shard_map/ppermute | solution.py:617
  9.4 2.6 %collective-permute-start.2 = (f32[45,8,128]{2,1,0:T(8,128)S(1)}, f32[45,8,128]{2,1,0:T(8,128)S(1)}, u32[]{:S(2)}, u32[]{:S(2)}) collective-permute-start(f32[45,8,128]{2,1,0:T(8,128)S(1)} %get-tuple-element.24.after), channel_id=1, source_target_pairs={{0,1},{4,5},{8,9},{12,13},{16,17},{20,21},{24,25},{28,29},{1,0},{5... | collective-permute-start | bytes 552968 | tf_op jit(solution)/shard_map/ppermute | solution.py:616
  12.0 7.5 %interior.1 = (f32[5,32,8,512]{3,2,1,0:T(8,128)S(1)}, f32[5,4,8,512]{3,2,1,0:T(8,128)S(1)}, f32[6,4,8,640]{3,2,1,0:T(8,128)S(1)}, f32[5,4,8,640]{3,2,1,0:T(8,128...) custom-call(f32[6,48,8,512]{3,2,1,0:T(8,128)S(1)} %get-tuple-element.19.planes, ...), custom_call_target="tpu_custom_call" | custom-call | flops 100000000 | bytes 10000000 | tf_op jit(solution)/shard_map/interior/pallas_call | solution.py:623
  19.6 0.0 collective-permute-done.3.rows_b
  19.6 0.0 collective-permute-done.2.rows_a
  19.6 2.3 %edges.1 = (f32[2,4,64,512]{3,2,1,0:T(8,128)}, f32[4,64,512]{2,1,0:T(8,128)}, f32[2,4,64,512]{3,2,1,0:T(8,128)}) custom-call(f32[6,4,8,640]{3,2,1,0:T(8,128)S(1)} %get-tuple-element.25.joint, f32[5,4,8,640]{3,2,1,0:T(8,128)S(1)} %get-tuple-element.26.ring, f32[2,5,2,8,640]{4,3,2,1,0:T(8,128)S(1)} %get-tuple-element.27.joint_sums, ...), custom_call_target="tpu_custom_call" | custom-call | flops 100000000 | bytes 10000000 | tf_op jit(solution)/shard_map/edges/pallas_call | solution.py:647
Async XLA Ops:
  2.4 6.2 %collective-permute-start.1 = (f32[6,8,128]{2,1,0:T(8,128)S(1)}, f32[6,8,128]{2,1,0:T(8,128)S(1)}, u32[]{:S(2)}, u32[]{:S(2)}) collective-permute-start(f32[6,8,128]{2,1,0:T(8,128)S(1)} %get-tuple-element.22), channel_id=1, source_target_pairs={{0,28},{4,8},{8,4},{12,16},{16,12},{20,24},{24,20},{28,0},{1,29},{... | collective-permute-start | bytes 73736 | tf_op jit(solution)/shard_map/ppermute | solution.py:592
  5.8 2.8 %collective-permute-start = (f32[6,8,128]{2,1,0:T(8,128)S(1)}, f32[6,8,128]{2,1,0:T(8,128)S(1)}, u32[]{:S(2)}, u32[]{:S(2)}) collective-permute-start(f32[6,8,128]{2,1,0:T(8,128)S(1)} %get-tuple-element.18.after), channel_id=1, source_target_pairs={{0,4},{4,0},{8,12},{12,8},{16,20},{20,16},{24,28},{28,24},{1,5},{5... | collective-permute-start | bytes 73736 | tf_op jit(solution)/shard_map/ppermute | solution.py:591
  8.8 10.8 %collective-permute-start.3 = (f32[45,8,128]{2,1,0:T(8,128)S(1)}, f32[45,8,128]{2,1,0:T(8,128)S(1)}, u32[]{:S(2)}, u32[]{:S(2)}) collective-permute-start(f32[45,8,128]{2,1,0:T(8,128)S(1)} %get-tuple-element.32), channel_id=1, source_target_pairs={{0,4},{4,0},{8,12},{12,8},{16,20},{20,16},{24,28},{28,24},{1,2},{5... | collective-permute-start | bytes 552968 | tf_op jit(solution)/shard_map/ppermute | solution.py:617
  9.4 10.2 %collective-permute-start.2 = (f32[45,8,128]{2,1,0:T(8,128)S(1)}, f32[45,8,128]{2,1,0:T(8,128)S(1)}, u32[]{:S(2)}, u32[]{:S(2)}) collective-permute-start(f32[45,8,128]{2,1,0:T(8,128)S(1)} %get-tuple-element.24.after), channel_id=1, source_target_pairs={{0,1},{4,5},{8,9},{12,13},{16,17},{20,21},{24,25},{28,29},{1,0},{5... | collective-permute-start | bytes 552968 | tf_op jit(solution)/shard_map/ppermute | solution.py:616

commit v5 on v4

--- a/solution.py
+++ b/solution.py
@@ -201,10 +201,10 @@
     def shifts(value):
         return pltpu.roll(value, wide - 1, 1), pltpu.roll(value, 1, 1)
 
-    def ahead(source, row, at, f, shifted):
+    def ahead(source, row, at, f, shifted, cut):
         to_east, to_west = shifted(f, row) if shifted else shifts(source(f, row))
         sums[f, at] = (to_east + to_west) + (source(f, row + 1) + source(f, row - 1))
-        east_diff[f, at] = to_east - to_west
+        east_diff[f, at, :, :cut] = (to_east - to_west)[:, :cut]
 
     def weighed_down(thick, temp, salt):
         lanes = slice(0, thick.shape[-1])
@@ -212,8 +212,8 @@
         part = part + jnp.where(below_one[:, lanes], pltpu.roll(part, 2, 0), 0.0)
         return part + jnp.where(below_two[:, lanes], pltpu.roll(part, 4, 0), 0.0)
 
-    def ahead_press(source, row, at):
-        press[at] = weighed_down(source(2, row), source(3, row), source(4, row))
+    def ahead_press(source, row, at, cut):
+        press[at, :, :cut] = weighed_down(*(source(f, row)[:, :cut] for f in (2, 3, 4)))
 
     def update_row(source, ocean, turn, row, at, cut, emit, northward=None, roll_press=False):
         lanes = slice(0, cut)
@@ -255,10 +255,10 @@
         for f in range(5):
             one(f)
 
-    def ahead_row(source, row, at, shifted=None):
-        ahead_press(source, row, at)
+    def ahead_row(source, row, at, cut, shifted=None):
+        ahead_press(source, row, at, cut)
         for f in range(5):
-            ahead(source, row, at, f, shifted)
+            ahead(source, row, at, f, shifted, cut)
 
     return ahead_row, update_row
 
@@ -336,13 +336,13 @@
         out[f, row] = value
 
     def sweep(source, low, high, cut, emit, shifted=None):
-        ahead_row(source, low - 1, low - 1 + PAD, shifted)
-        ahead_row(source, low, low + PAD, shifted)
+        ahead_row(source, low - 1, low - 1 + PAD, cut, shifted)
+        ahead_row(source, low, low + PAD, cut, shifted)
 
         def iteration(row, carry):
             if shifted:
                 add_halo(row + 2)
-            ahead_row(source, row + 1, row + 1 + PAD, shifted)
+            ahead_row(source, row + 1, row + 1 + PAD, cut, shifted)
             ocean, turn = whole(5, row)[:, :cut], coriolis[row + PAD]
             update_row(source, ocean, turn, row, row + PAD, cut, emit, roll_press=bool(shifted))
             return carry
@@ -401,7 +401,7 @@
         centre[f, i + 2] = value
         centre[f, 1 - i] = swap_halves(value)
 
-    ahead_row(mirrored, 0, 1, mirrored_shifted)
+    ahead_row(mirrored, 0, 1, wide, mirrored_shifted)
     fold_inner()
     take_inner(1)
     take_inner(2)
@@ -418,7 +418,7 @@
         middle[f, i] = value
 
     for i in range(3):
-        ahead_row(centre_halfway, i, i + 1)
+        ahead_row(centre_halfway, i, i + 1, width)
     fold_inner()
     take_inner(3)
     take_inner(4)
@@ -521,11 +521,11 @@
             press[high - 1 + k + 4] = joint_press[step, k]
         for f in range(5):
             east_diff[f, high - 1 + 4] = joint_diff[step, f]
-        ahead_row(source, low - 1, low + 3)
-        ahead_row(source, low, low + 4)
+        ahead_row(source, low - 1, low + 3, cut)
+        ahead_row(source, low, low + 4, cut)
         for i in range(low, high):
             if i + 1 < high - 1:
-                ahead_row(source, i + 1, i + 5)
+                ahead_row(source, i + 1, i + 5, cut)
             turn = jnp.where(even_one, coriolis[i + PAD], coriolis[half_rows - 1 - i + PAD])
             update_row(source, whole(5, i)[:, :cut], turn, i, i + 4, cut, emit, north_even)
 
@@ -642,7 +642,7 @@
             *work(tall),
         ],
         10**8,
-    )(planes, from_east, from_west, cols_a, cols_b, coriolis, send_a)
+    )(planes, from_east, from_west, cols_a, cols_b, coriolis, send_b)
 
     return call(
         edges_kernel,

time: 22.2 us -> 21 us (0.946)
  starting transfers between devices: 6.62 us -> 5.27 us
    ppermute x1, starting transfers between devices: 2.65 us -> 1.64 us  [body(): rows_a = lax.ppermute(send_a, axes, lat_pairs(0, lat_count, lon_count))]
    ppermute x1, starting transfers between devices: 0.57 us -> 0.22 us  [body(): rows_b = lax.ppermute(send_b, axes, lat_pairs(1, lat_count, lon_count))]
  transfers between devices with their start and end apart: 4 -> 4, of which waited for: 0 -> 0; matrix products, arithmetic and copies ran while one was open for 0% -> 0% of each run, Pallas kernels for 47% -> 50%
where the time goes in v5:
time: 21 us; the launch traced here: 20.6 us
  Pallas kernels  14.6 us (70%)
  starting transfers between devices  5.27 us (25%)
  between operations  0.69 us (3%)
    pallas_call x1, Pallas kernels, body(): call(interior_kernel, 'interior', [VMEM] * 6 + [ANY], (shapes(5, half_row...  7.52 us
    ppermute x1, starting transfers between devices, body(): cols_b = lax.ppermute(send_b, 'lon', lon_pairs(1, lon_count))  3.4 us
    pallas_call x1, Pallas kernels, body(): call(functools.partial(load_kernel, lat_count), 'load_fields', [HBM, HBM,...  2.78 us
    pallas_call x1, Pallas kernels, body(): call(edges_kernel, 'edges', [VMEM] * 10, (shapes(*velocity.shape), shapes...  2.34 us
    pallas_call x1, Pallas kernels, body(): call(columns_kernel, 'pack_columns', [HBM] * 4, (columns, columns), (VMEM...  1.74 us
    ppermute x1, starting transfers between devices, body(): rows_a = lax.ppermute(send_a, axes, lat_pairs(0, lat_count, lon_count))  1.64 us
  transfers between devices with their start and end apart: 4, of which 0 were waited for; matrix products, arithmetic and copies ran while one was open for 0% of the time, Pallas kernels for 50%

profile of v5, /device:TPU:0, one launch (start us, length us, event | category | flops | bytes accessed | tf_op | source)
XLA Modules:
  0.0 20.6 jit_solution(14498787928400544267)
XLA Ops:
  0.6 1.7 %pack_columns.1 = (f32[6,8,128]{2,1,0:T(8,128)S(1)}, f32[6,8,128]{2,1,0:T(8,128)S(1)}) custom-call(f32[2,4,64,512]{3,2,1,0:T(8,128)} %vel.3, f32[4,64,512]{2,1,0:T(8,128)} %thick.3, f32[2,4,64,512]{3,2,1,0:T(8,128)} %trac.3, s32[4,64,512]{2,1,0:T(8,128)} %mask.3), custom_call_target="tpu_custom_call" | custom-call | flops 1000000 | bytes 100000 | tf_op jit(solution)/shard_map/pack_columns/pallas_call | solution.py:582
  2.4 3.4 %collective-permute-start.1 = (f32[6,8,128]{2,1,0:T(8,128)S(1)}, f32[6,8,128]{2,1,0:T(8,128)S(1)}, u32[]{:S(2)}, u32[]{:S(2)}) collective-permute-start(f32[6,8,128]{2,1,0:T(8,128)S(1)} %get-tuple-element.22), channel_id=1, source_target_pairs={{0,28},{4,8},{8,4},{12,16},{16,12},{20,24},{24,20},{28,0},{1,29},{... | collective-permute-start | bytes 73736 | tf_op jit(solution)/shard_map/ppermute | solution.py:592
  5.8 0.0 collective-permute-start
  5.8 2.8 %load_fields.1 = (f32[6,48,8,512]{3,2,1,0:T(8,128)S(1)}, f32[4,48,8,512]{3,2,1,0:T(8,128)S(1)}, f32[4,48,8,512]{3,2,1,0:T(8,128)S(1)}, f32[48,8,128]{2,1,0:T(8,128)S(1)}) custom-call(f32[2,4,64,512]{3,2,1,0:T(8,128)} %vel.3, f32[4,64,512]{2,1,0:T(8,128)} %thick.3, f32[2,4,64,512]{3,2,1,0:T(8,128)} %trac.3, s32[4,64,512]{2,1,0:T(8,128)} %mask.3, ...), custom_call_target="tpu_custom_call" | custom-call | flops 100000000 | bytes 10000000 | tf_op jit(solution)/shard_map/load_fields/pallas_call | solution.py:595
  8.6 0.0 collective-permute-done.1.cols_b
  8.6 0.0 collective-permute-done.cols_a
  8.6 0.2 %pack_rows.1 = (f32[45,8,128]{2,1,0:T(8,128)S(1)}, f32[45,8,128]{2,1,0:T(8,128)S(1)}) custom-call(f32[6,48,8,512]{3,2,1,0:T(8,128)S(1)} %get-tuple-element.19.planes, f32[6,8,128]{2,1,0:T(8,128)S(1)} %collective-permute-done.cols_a, f32[6,8,128]{2,1,0:T(8,128)S(1)} %collective-permute-done.1.cols_b), custom_call_target="tpu_custom_call" | custom-call | flops 1000000 | bytes 100000 | tf_op jit(solution)/shard_map/pack_rows/pallas_call | solution.py:606
  8.8 1.6 %collective-permute-start.2 = (f32[45,8,128]{2,1,0:T(8,128)S(1)}, f32[45,8,128]{2,1,0:T(8,128)S(1)}, u32[]{:S(2)}, u32[]{:S(2)}) collective-permute-start(f32[45,8,128]{2,1,0:T(8,128)S(1)} %get-tuple-element.32), channel_id=1, source_target_pairs={{0,1},{4,5},{8,9},{12,13},{16,17},{20,21},{24,25},{28,29},{1,0},{5... | collective-permute-start | bytes 552968 | tf_op jit(solution)/shard_map/ppermute | solution.py:616
  10.5 0.2 %collective-permute-start.3 = (f32[45,8,128]{2,1,0:T(8,128)S(1)}, f32[45,8,128]{2,1,0:T(8,128)S(1)}, u32[]{:S(2)}, u32[]{:S(2)}) collective-permute-start(f32[45,8,128]{2,1,0:T(8,128)S(1)} %get-tuple-element.24.after), channel_id=1, source_target_pairs={{0,4},{4,0},{8,12},{12,8},{16,20},{20,16},{24,28},{28,24},{1,2},{5... | collective-permute-start | bytes 552968 | tf_op jit(solution)/shard_map/ppermute | solution.py:617
  10.7 7.5 %interior.1 = (f32[5,32,8,512]{3,2,1,0:T(8,128)S(1)}, f32[5,4,8,512]{3,2,1,0:T(8,128)S(1)}, f32[6,4,8,640]{3,2,1,0:T(8,128)S(1)}, f32[5,4,8,640]{3,2,1,0:T(8,128...) custom-call(f32[6,48,8,512]{3,2,1,0:T(8,128)S(1)} %get-tuple-element.19.planes, ...), custom_call_target="tpu_custom_call" | custom-call | flops 100000000 | bytes 10000000 | tf_op jit(solution)/shard_map/interior/pallas_call | solution.py:623
  18.2 0.0 collective-permute-done.2.rows_a
  18.2 0.0 collective-permute-done.3.rows_b
  18.2 2.3 %edges.1 = (f32[2,4,64,512]{3,2,1,0:T(8,128)}, f32[4,64,512]{2,1,0:T(8,128)}, f32[2,4,64,512]{3,2,1,0:T(8,128)}) custom-call(f32[6,4,8,640]{3,2,1,0:T(8,128)S(1)} %get-tuple-element.25.joint, f32[5,4,8,640]{3,2,1,0:T(8,128)S(1)} %get-tuple-element.26.ring, f32[2,5,2,8,640]{4,3,2,1,0:T(8,128)S(1)} %get-tuple-element.27.joint_sums, ...), custom_call_target="tpu_custom_call" | custom-call | flops 100000000 | bytes 10000000 | tf_op jit(solution)/shard_map/edges/pallas_call | solution.py:647
Async XLA Ops:
  2.4 6.2 %collective-permute-start.1 = (f32[6,8,128]{2,1,0:T(8,128)S(1)}, f32[6,8,128]{2,1,0:T(8,128)S(1)}, u32[]{:S(2)}, u32[]{:S(2)}) collective-permute-start(f32[6,8,128]{2,1,0:T(8,128)S(1)} %get-tuple-element.22), channel_id=1, source_target_pairs={{0,28},{4,8},{8,4},{12,16},{16,12},{20,24},{24,20},{28,0},{1,29},{... | collective-permute-start | bytes 73736 | tf_op jit(solution)/shard_map/ppermute | solution.py:592
  5.8 2.8 %collective-permute-start = (f32[6,8,128]{2,1,0:T(8,128)S(1)}, f32[6,8,128]{2,1,0:T(8,128)S(1)}, u32[]{:S(2)}, u32[]{:S(2)}) collective-permute-start(f32[6,8,128]{2,1,0:T(8,128)S(1)} %get-tuple-element.18.after), channel_id=1, source_target_pairs={{0,4},{4,0},{8,12},{12,8},{16,20},{20,16},{24,28},{28,24},{1,5},{5... | collective-permute-start | bytes 73736 | tf_op jit(solution)/shard_map/ppermute | solution.py:591
  8.8 9.4 %collective-permute-start.2 = (f32[45,8,128]{2,1,0:T(8,128)S(1)}, f32[45,8,128]{2,1,0:T(8,128)S(1)}, u32[]{:S(2)}, u32[]{:S(2)}) collective-permute-start(f32[45,8,128]{2,1,0:T(8,128)S(1)} %get-tuple-element.32), channel_id=1, source_target_pairs={{0,1},{4,5},{8,9},{12,13},{16,17},{20,21},{24,25},{28,29},{1,0},{5... | collective-permute-start | bytes 552968 | tf_op jit(solution)/shard_map/ppermute | solution.py:616
  10.5 7.8 %collective-permute-start.3 = (f32[45,8,128]{2,1,0:T(8,128)S(1)}, f32[45,8,128]{2,1,0:T(8,128)S(1)}, u32[]{:S(2)}, u32[]{:S(2)}) collective-permute-start(f32[45,8,128]{2,1,0:T(8,128)S(1)} %get-tuple-element.24.after), channel_id=1, source_target_pairs={{0,4},{4,0},{8,12},{12,8},{16,20},{20,16},{24,28},{28,24},{1,2},{5... | collective-permute-start | bytes 552968 | tf_op jit(solution)/shard_map/ppermute | solution.py:617

commit v6 on v5

--- a/solution.py
+++ b/solution.py
@@ -76,12 +76,11 @@
     del after
     levels, rows, width = thick.shape
     half_rows = rows // 2
-    length = half_rows + PAD
     groups = {0: [], 2: [], 3: [], 5: []}
     for level in range(levels):
         for half in range(2):
-            at, s = pl.ds(half * (half_rows - PAD), length), 2 * level + half
-            to = pl.ds((1 - half) * PAD, length)
+            at, s = pl.ds(half * half_rows, half_rows), 2 * level + half
+            to = pl.ds(PAD, half_rows)
             for f, source, target in (
                 (0, vel.at[:, level, at, :], planes.at[0:2, to, s, :]),
                 (2, thick.at[level, at, :], planes.at[2, to, s, :]),
@@ -109,7 +108,7 @@
             value = planes[f, row]
             from_east[f, row] = pltpu.roll(value, width - 1, 1)
             from_west[f, row] = pltpu.roll(value, 1, 1)
-    for row in range(PAD - 2, half_rows + PAD + 2):
+    for row in range(PAD, half_rows + PAD):
         planes[5, row] = HYPERVISCOSITY * land[row].astype(F32)
 
 
@@ -215,7 +214,7 @@
     def ahead_press(source, row, at, cut):
         press[at, :, :cut] = weighed_down(*(source(f, row)[:, :cut] for f in (2, 3, 4)))
 
-    def update_row(source, ocean, turn, row, at, cut, emit, northward=None, roll_press=False):
+    def update_row(source, ocean, turn, row, at, cut, emit, northward=None, roll_press=False, fields=range(5)):
         lanes = slice(0, cut)
         turn = jnp.concatenate([turn] * (cut // LANES), axis=1)
         u, v = source(0, row)[:, lanes], source(1, row)[:, lanes]
@@ -252,7 +251,7 @@
                 value = value + add_on(f)
             emit(f, row, value * ocean)
 
-        for f in range(5):
+        for f in fields:
             one(f)
 
     def ahead_row(source, row, at, cut, shifted=None):
@@ -375,9 +374,6 @@
         press[0] = swap_halves(press[1])
 
     sweep(whole, 2, half_rows - 2, wide, keep, whole_shifted)
-    for f in range(5):
-        outer[f, half_rows + PAD] = pltpu.roll(outer[f, PAD], SUB - 1, 0)
-        outer[f, PAD - 1] = pltpu.roll(outer[f, last + PAD], 1, 0)
     save_outer(0, 1)
     for i in range(4):
         for f in range(6):
@@ -386,6 +382,8 @@
             ring[f, i] = outer_pair(second.at[f], 2 + i)
 
     def mirrored(f, i):
+        if i < 0:
+            return swap_halves(mirrored(f, -1 - i))
         return jnp.where(even, whole(f, last - i), whole(f, i))
 
     def mirrored_shifted(f, i):
@@ -454,17 +452,18 @@
     chunks = width // LANES
     levels = SUB // 2
 
-    def copies_out(source, source_row, row, count):
+    def copies_out(source, source_row, row, count, groups=(0, 2, 3)):
         copies = []
         for level in range(levels):
             for half in range(2):
                 s = 2 * level + half
                 rows, to = pl.ds(source_row, count), pl.ds(half * half_rows + row, count)
-                copies += [
-                    pltpu.make_async_copy(source.at[0:2, rows, s, :], vel_out.at[:, level, to, :], sem),
-                    pltpu.make_async_copy(source.at[2, rows, s, :], thick_out.at[level, to, :], sem),
-                    pltpu.make_async_copy(source.at[3:5, rows, s, :], trac_out.at[:, level, to, :], sem),
-                ]
+                ends = {
+                    0: (source.at[0:2, rows, s, :], vel_out.at[:, level, to, :]),
+                    2: (source.at[2, rows, s, :], thick_out.at[level, to, :]),
+                    3: (source.at[3:5, rows, s, :], trac_out.at[:, level, to, :]),
+                }
+                copies += [pltpu.make_async_copy(*ends[group], sem) for group in groups]
         for copy in copies:
             copy.start()
         return copies
@@ -521,18 +520,21 @@
             press[high - 1 + k + 4] = joint_press[step, k]
         for f in range(5):
             east_diff[f, high - 1 + 4] = joint_diff[step, f]
-        ahead_row(source, low - 1, low + 3, cut)
-        ahead_row(source, low, low + 4, cut)
-        for i in range(low, high):
-            if i + 1 < high - 1:
-                ahead_row(source, i + 1, i + 5, cut)
-            turn = jnp.where(even_one, coriolis[i + PAD], coriolis[half_rows - 1 - i + PAD])
-            update_row(source, whole(5, i)[:, :cut], turn, i, i + 4, cut, emit, north_even)
+        for i in range(low - 1, low + 3):
+            ahead_row(source, i, i + 4, cut)
+        sent = []
+        for fields in ((0, 1, 2, 3, 4),) if step == 0 else ((0, 1), (2,), (3, 4)):
+            for i in range(low, high):
+                turn = jnp.where(even_one, coriolis[i + PAD], coriolis[half_rows - 1 - i + PAD])
+                ocean = whole(5, i)[:, :cut]
+                update_row(source, ocean, turn, i, i + 4, cut, emit, north_even, fields=fields)
+            if step == 1:
+                sent += copies_out(strip, 0, 0, PAD, fields[:1])
+                sent += copies_out(strip, PAD, half_rows - PAD, PAD, fields[:1])
+        return sent
 
     sweep(whole, 0, -2, wide, keep)
-    sweep(halfway, 1, 0, width, write)
-    copies += copies_out(strip, 0, 0, PAD)
-    copies += copies_out(strip, PAD, half_rows - PAD, PAD)
+    copies += sweep(halfway, 1, 0, width, write)
     for copy in copies:
         copy.wait()
 

time: 21 us -> 20.8 us (level)
  no operation moved by 1% of the time
where the time goes in v6:
time: 20.8 us; the launch traced here: 20.4 us
  Pallas kernels  14.4 us (69%)
  starting transfers between devices  5.27 us (25%)
  between operations  0.69 us (3%)
    pallas_call x1, Pallas kernels, body(): call(interior_kernel, 'interior', [VMEM] * 6 + [ANY], (shapes(5, half_row...  7.52 us
    ppermute x1, starting transfers between devices, body(): cols_b = lax.ppermute(send_b, 'lon', lon_pairs(1, lon_count))  3.4 us
    pallas_call x1, Pallas kernels, body(): call(functools.partial(load_kernel, lat_count), 'load_fields', [HBM, HBM,...  2.67 us
    pallas_call x1, Pallas kernels, body(): call(edges_kernel, 'edges', [VMEM] * 10, (shapes(*velocity.shape), shapes...  2.23 us
    pallas_call x1, Pallas kernels, body(): call(columns_kernel, 'pack_columns', [HBM] * 4, (columns, columns), (VMEM...  1.74 us
    ppermute x1, starting transfers between devices, body(): rows_a = lax.ppermute(send_a, axes, lat_pairs(0, lat_count, lon_count))  1.64 us
  transfers between devices with their start and end apart: 4, of which 0 were waited for; matrix products, arithmetic and copies ran while one was open for 0% of the time, Pallas kernels for 50%

profile of v6, /device:TPU:0, one launch (start us, length us, event | category | flops | bytes accessed | tf_op | source)
XLA Modules:
  0.0 20.4 jit_solution(6035465055731903296)
XLA Ops:
  0.6 1.7 %pack_columns.1 = (f32[6,8,128]{2,1,0:T(8,128)S(1)}, f32[6,8,128]{2,1,0:T(8,128)S(1)}) custom-call(f32[2,4,64,512]{3,2,1,0:T(8,128)} %vel.3, f32[4,64,512]{2,1,0:T(8,128)} %thick.3, f32[2,4,64,512]{3,2,1,0:T(8,128)} %trac.3, s32[4,64,512]{2,1,0:T(8,128)} %mask.3), custom_call_target="tpu_custom_call" | custom-call | flops 1000000 | bytes 100000 | tf_op jit(solution)/shard_map/pack_columns/pallas_call | solution.py:584
  2.4 3.4 %collective-permute-start.1 = (f32[6,8,128]{2,1,0:T(8,128)S(1)}, f32[6,8,128]{2,1,0:T(8,128)S(1)}, u32[]{:S(2)}, u32[]{:S(2)}) collective-permute-start(f32[6,8,128]{2,1,0:T(8,128)S(1)} %get-tuple-element.22), channel_id=1, source_target_pairs={{0,28},{4,8},{8,4},{12,16},{16,12},{20,24},{24,20},{28,0},{1,29},{... | collective-permute-start | bytes 73736 | tf_op jit(solution)/shard_map/ppermute | solution.py:594
  5.8 0.0 collective-permute-start
  5.8 2.7 %load_fields.1 = (f32[6,48,8,512]{3,2,1,0:T(8,128)S(1)}, f32[4,48,8,512]{3,2,1,0:T(8,128)S(1)}, f32[4,48,8,512]{3,2,1,0:T(8,128)S(1)}, f32[48,8,128]{2,1,0:T(8,128)S(1)}) custom-call(f32[2,4,64,512]{3,2,1,0:T(8,128)} %vel.3, f32[4,64,512]{2,1,0:T(8,128)} %thick.3, f32[2,4,64,512]{3,2,1,0:T(8,128)} %trac.3, s32[4,64,512]{2,1,0:T(8,128)} %mask.3, ...), custom_call_target="tpu_custom_call" | custom-call | flops 100000000 | bytes 10000000 | tf_op jit(solution)/shard_map/load_fields/pallas_call | solution.py:597
  8.5 0.0 collective-permute-done.1.cols_b
  8.5 0.0 collective-permute-done.cols_a
  8.5 0.2 %pack_rows.1 = (f32[45,8,128]{2,1,0:T(8,128)S(1)}, f32[45,8,128]{2,1,0:T(8,128)S(1)}) custom-call(f32[6,48,8,512]{3,2,1,0:T(8,128)S(1)} %get-tuple-element.19.planes, f32[6,8,128]{2,1,0:T(8,128)S(1)} %collective-permute-done.cols_a, f32[6,8,128]{2,1,0:T(8,128)S(1)} %collective-permute-done.1.cols_b), custom_call_target="tpu_custom_call" | custom-call | flops 1000000 | bytes 100000 | tf_op jit(solution)/shard_map/pack_rows/pallas_call | solution.py:608
  8.7 1.6 %collective-permute-start.2 = (f32[45,8,128]{2,1,0:T(8,128)S(1)}, f32[45,8,128]{2,1,0:T(8,128)S(1)}, u32[]{:S(2)}, u32[]{:S(2)}) collective-permute-start(f32[45,8,128]{2,1,0:T(8,128)S(1)} %get-tuple-element.32), channel_id=1, source_target_pairs={{0,1},{4,5},{8,9},{12,13},{16,17},{20,21},{24,25},{28,29},{1,0},{5... | collective-permute-start | bytes 552968 | tf_op jit(solution)/shard_map/ppermute | solution.py:618
  10.4 0.2 %collective-permute-start.3 = (f32[45,8,128]{2,1,0:T(8,128)S(1)}, f32[45,8,128]{2,1,0:T(8,128)S(1)}, u32[]{:S(2)}, u32[]{:S(2)}) collective-permute-start(f32[45,8,128]{2,1,0:T(8,128)S(1)} %get-tuple-element.24.after), channel_id=1, source_target_pairs={{0,4},{4,0},{8,12},{12,8},{16,20},{20,16},{24,28},{28,24},{1,2},{5... | collective-permute-start | bytes 552968 | tf_op jit(solution)/shard_map/ppermute | solution.py:619
  10.6 7.5 %interior.1 = (f32[5,32,8,512]{3,2,1,0:T(8,128)S(1)}, f32[5,4,8,512]{3,2,1,0:T(8,128)S(1)}, f32[6,4,8,640]{3,2,1,0:T(8,128)S(1)}, f32[5,4,8,640]{3,2,1,0:T(8,128...) custom-call(f32[6,48,8,512]{3,2,1,0:T(8,128)S(1)} %get-tuple-element.19.planes, ...), custom_call_target="tpu_custom_call" | custom-call | flops 100000000 | bytes 10000000 | tf_op jit(solution)/shard_map/interior/pallas_call | solution.py:625
  18.1 0.0 collective-permute-done.2.rows_a
  18.1 0.0 collective-permute-done.3.rows_b
  18.1 2.2 %edges.1 = (f32[2,4,64,512]{3,2,1,0:T(8,128)}, f32[4,64,512]{2,1,0:T(8,128)}, f32[2,4,64,512]{3,2,1,0:T(8,128)}) custom-call(f32[6,4,8,640]{3,2,1,0:T(8,128)S(1)} %get-tuple-element.25.joint, f32[5,4,8,640]{3,2,1,0:T(8,128)S(1)} %get-tuple-element.26.ring, f32[2,5,2,8,640]{4,3,2,1,0:T(8,128)S(1)} %get-tuple-element.27.joint_sums, ...), custom_call_target="tpu_custom_call" | custom-call | flops 100000000 | bytes 10000000 | tf_op jit(solution)/shard_map/edges/pallas_call | solution.py:649
Async XLA Ops:
  2.4 6.1 %collective-permute-start.1 = (f32[6,8,128]{2,1,0:T(8,128)S(1)}, f32[6,8,128]{2,1,0:T(8,128)S(1)}, u32[]{:S(2)}, u32[]{:S(2)}) collective-permute-start(f32[6,8,128]{2,1,0:T(8,128)S(1)} %get-tuple-element.22), channel_id=1, source_target_pairs={{0,28},{4,8},{8,4},{12,16},{16,12},{20,24},{24,20},{28,0},{1,29},{... | collective-permute-start | bytes 73736 | tf_op jit(solution)/shard_map/ppermute | solution.py:594
  5.8 2.7 %collective-permute-start = (f32[6,8,128]{2,1,0:T(8,128)S(1)}, f32[6,8,128]{2,1,0:T(8,128)S(1)}, u32[]{:S(2)}, u32[]{:S(2)}) collective-permute-start(f32[6,8,128]{2,1,0:T(8,128)S(1)} %get-tuple-element.18.after), channel_id=1, source_target_pairs={{0,4},{4,0},{8,12},{12,8},{16,20},{20,16},{24,28},{28,24},{1,5},{5... | collective-permute-start | bytes 73736 | tf_op jit(solution)/shard_map/ppermute | solution.py:593
  8.7 9.4 %collective-permute-start.2 = (f32[45,8,128]{2,1,0:T(8,128)S(1)}, f32[45,8,128]{2,1,0:T(8,128)S(1)}, u32[]{:S(2)}, u32[]{:S(2)}) collective-permute-start(f32[45,8,128]{2,1,0:T(8,128)S(1)} %get-tuple-element.32), channel_id=1, source_target_pairs={{0,1},{4,5},{8,9},{12,13},{16,17},{20,21},{24,25},{28,29},{1,0},{5... | collective-permute-start | bytes 552968 | tf_op jit(solution)/shard_map/ppermute | solution.py:618
  10.4 7.8 %collective-permute-start.3 = (f32[45,8,128]{2,1,0:T(8,128)S(1)}, f32[45,8,128]{2,1,0:T(8,128)S(1)}, u32[]{:S(2)}, u32[]{:S(2)}) collective-permute-start(f32[45,8,128]{2,1,0:T(8,128)S(1)} %get-tuple-element.24.after), channel_id=1, source_target_pairs={{0,4},{4,0},{8,12},{12,8},{16,20},{20,16},{24,28},{28,24},{1,2},{5... | collective-permute-start | bytes 552968 | tf_op jit(solution)/shard_map/ppermute | solution.py:619

commit v7 on v6

--- a/solution.py
+++ b/solution.py
@@ -19,7 +19,7 @@
 LANES = 128
 SUB = 8
 SLOTS = 11
-ROLLED = 4
+ROLLED = 3
 F32 = jnp.float32
 VMEM = pl.BlockSpec(memory_space=pltpu.VMEM)
 HBM = pl.BlockSpec(memory_space=pltpu.HBM)

time: 20.8 us -> 20.5 us (0.986)
  Pallas kernels: 14.4 us -> 14.1 us
    pallas_call x1, Pallas kernels: 2.67 us -> 2.34 us  [body(): call(functools.partial(load_kernel, lat_count), 'load_fields', [HBM, HBM,...]
where the time goes in v7:
time: 20.5 us; the launch traced here: 20.1 us
  Pallas kernels  14.1 us (69%)
  starting transfers between devices  5.27 us (26%)
  between operations  0.69 us (3%)
    pallas_call x1, Pallas kernels, body(): call(interior_kernel, 'interior', [VMEM] * 6 + [ANY], (shapes(5, half_row...  7.65 us
    ppermute x1, starting transfers between devices, body(): cols_b = lax.ppermute(send_b, 'lon', lon_pairs(1, lon_count))  3.4 us
    pallas_call x1, Pallas kernels, body(): call(functools.partial(load_kernel, lat_count), 'load_fields', [HBM, HBM,...  2.34 us
    pallas_call x1, Pallas kernels, body(): call(edges_kernel, 'edges', [VMEM] * 10, (shapes(*velocity.shape), shapes...  2.17 us
    pallas_call x1, Pallas kernels, body(): call(columns_kernel, 'pack_columns', [HBM] * 4, (columns, columns), (VMEM...  1.74 us
    ppermute x1, starting transfers between devices, body(): rows_a = lax.ppermute(send_a, axes, lat_pairs(0, lat_count, lon_count))  1.69 us
  transfers between devices with their start and end apart: 4, of which 0 were waited for; matrix products, arithmetic and copies ran while one was open for 0% of the time, Pallas kernels for 50%

profile of v7, /device:TPU:0, one launch (start us, length us, event | category | flops | bytes accessed | tf_op | source)
XLA Modules:
  0.0 20.1 jit_solution(12502423261220617594)
XLA Ops:
  0.6 1.7 %pack_columns.1 = (f32[6,8,128]{2,1,0:T(8,128)S(1)}, f32[6,8,128]{2,1,0:T(8,128)S(1)}) custom-call(f32[2,4,64,512]{3,2,1,0:T(8,128)} %vel.3, f32[4,64,512]{2,1,0:T(8,128)} %thick.3, f32[2,4,64,512]{3,2,1,0:T(8,128)} %trac.3, s32[4,64,512]{2,1,0:T(8,128)} %mask.3), custom_call_target="tpu_custom_call" | custom-call | flops 1000000 | bytes 100000 | tf_op jit(solution)/shard_map/pack_columns/pallas_call | solution.py:584
  2.4 3.4 %collective-permute-start.1 = (f32[6,8,128]{2,1,0:T(8,128)S(1)}, f32[6,8,128]{2,1,0:T(8,128)S(1)}, u32[]{:S(2)}, u32[]{:S(2)}) collective-permute-start(f32[6,8,128]{2,1,0:T(8,128)S(1)} %get-tuple-element.22), channel_id=1, source_target_pairs={{0,28},{4,8},{8,4},{12,16},{16,12},{20,24},{24,20},{28,0},{1,29},{... | collective-permute-start | bytes 73736 | tf_op jit(solution)/shard_map/ppermute | solution.py:594
  5.8 0.0 collective-permute-start
  5.8 2.3 %load_fields.1 = (f32[6,48,8,512]{3,2,1,0:T(8,128)S(1)}, f32[3,48,8,512]{3,2,1,0:T(8,128)S(1)}, f32[3,48,8,512]{3,2,1,0:T(8,128)S(1)}, f32[48,8,128]{2,1,0:T(8,128)S(1)}) custom-call(f32[2,4,64,512]{3,2,1,0:T(8,128)} %vel.3, f32[4,64,512]{2,1,0:T(8,128)} %thick.3, f32[2,4,64,512]{3,2,1,0:T(8,128)} %trac.3, s32[4,64,512]{2,1,0:T(8,128)} %mask.3, ...), custom_call_target="tpu_custom_call" | custom-call | flops 100000000 | bytes 10000000 | tf_op jit(solution)/shard_map/load_fields/pallas_call | solution.py:597
  8.1 0.0 collective-permute-done.1.cols_b
  8.1 0.0 collective-permute-done.cols_a
  8.1 0.2 %pack_rows.1 = (f32[45,8,128]{2,1,0:T(8,128)S(1)}, f32[45,8,128]{2,1,0:T(8,128)S(1)}) custom-call(f32[6,48,8,512]{3,2,1,0:T(8,128)S(1)} %get-tuple-element.19.planes, f32[6,8,128]{2,1,0:T(8,128)S(1)} %collective-permute-done.cols_a, f32[6,8,128]{2,1,0:T(8,128)S(1)} %collective-permute-done.1.cols_b), custom_call_target="tpu_custom_call" | custom-call | flops 1000000 | bytes 100000 | tf_op jit(solution)/shard_map/pack_rows/pallas_call | solution.py:608
  8.4 1.7 %collective-permute-start.2 = (f32[45,8,128]{2,1,0:T(8,128)S(1)}, f32[45,8,128]{2,1,0:T(8,128)S(1)}, u32[]{:S(2)}, u32[]{:S(2)}) collective-permute-start(f32[45,8,128]{2,1,0:T(8,128)S(1)} %get-tuple-element.32), channel_id=1, source_target_pairs={{0,1},{4,5},{8,9},{12,13},{16,17},{20,21},{24,25},{28,29},{1,0},{5... | collective-permute-start | bytes 552968 | tf_op jit(solution)/shard_map/ppermute | solution.py:618
  10.1 0.2 collective-permute-start.3
  10.2 7.7 %interior.1 = (f32[5,32,8,512]{3,2,1,0:T(8,128)S(1)}, f32[5,4,8,512]{3,2,1,0:T(8,128)S(1)}, f32[6,4,8,640]{3,2,1,0:T(8,128)S(1)}, f32[5,4,8,640]{3,2,1,0:T(8,128...) custom-call(f32[6,48,8,512]{3,2,1,0:T(8,128)S(1)} %get-tuple-element.19.planes, ...), custom_call_target="tpu_custom_call" | custom-call | flops 100000000 | bytes 10000000 | tf_op jit(solution)/shard_map/interior/pallas_call | solution.py:625
  17.9 0.0 collective-permute-done.2.rows_a
  17.9 0.0 collective-permute-done.3.rows_b
  17.9 2.2 %edges.1 = (f32[2,4,64,512]{3,2,1,0:T(8,128)}, f32[4,64,512]{2,1,0:T(8,128)}, f32[2,4,64,512]{3,2,1,0:T(8,128)}) custom-call(f32[6,4,8,640]{3,2,1,0:T(8,128)S(1)} %get-tuple-element.25.joint, f32[5,4,8,640]{3,2,1,0:T(8,128)S(1)} %get-tuple-element.26.ring, f32[2,5,2,8,640]{4,3,2,1,0:T(8,128)S(1)} %get-tuple-element.27.joint_sums, ...), custom_call_target="tpu_custom_call" | custom-call | flops 100000000 | bytes 10000000 | tf_op jit(solution)/shard_map/edges/pallas_call | solution.py:649
Async XLA Ops:
  2.4 5.7 %collective-permute-start.1 = (f32[6,8,128]{2,1,0:T(8,128)S(1)}, f32[6,8,128]{2,1,0:T(8,128)S(1)}, u32[]{:S(2)}, u32[]{:S(2)}) collective-permute-start(f32[6,8,128]{2,1,0:T(8,128)S(1)} %get-tuple-element.22), channel_id=1, source_target_pairs={{0,28},{4,8},{8,4},{12,16},{16,12},{20,24},{24,20},{28,0},{1,29},{... | collective-permute-start | bytes 73736 | tf_op jit(solution)/shard_map/ppermute | solution.py:594
  5.8 2.4 %collective-permute-start = (f32[6,8,128]{2,1,0:T(8,128)S(1)}, f32[6,8,128]{2,1,0:T(8,128)S(1)}, u32[]{:S(2)}, u32[]{:S(2)}) collective-permute-start(f32[6,8,128]{2,1,0:T(8,128)S(1)} %get-tuple-element.18.after), channel_id=1, source_target_pairs={{0,4},{4,0},{8,12},{12,8},{16,20},{20,16},{24,28},{28,24},{1,5},{5... | collective-permute-start | bytes 73736 | tf_op jit(solution)/shard_map/ppermute | solution.py:593
  8.4 9.5 %collective-permute-start.2 = (f32[45,8,128]{2,1,0:T(8,128)S(1)}, f32[45,8,128]{2,1,0:T(8,128)S(1)}, u32[]{:S(2)}, u32[]{:S(2)}) collective-permute-start(f32[45,8,128]{2,1,0:T(8,128)S(1)} %get-tuple-element.32), channel_id=1, source_target_pairs={{0,1},{4,5},{8,9},{12,13},{16,17},{20,21},{24,25},{28,29},{1,0},{5... | collective-permute-start | bytes 552968 | tf_op jit(solution)/shard_map/ppermute | solution.py:618
  10.1 7.8 %collective-permute-start.3 = (f32[45,8,128]{2,1,0:T(8,128)S(1)}, f32[45,8,128]{2,1,0:T(8,128)S(1)}, u32[]{:S(2)}, u32[]{:S(2)}) collective-permute-start(f32[45,8,128]{2,1,0:T(8,128)S(1)} %get-tuple-element.24.after), channel_id=1, source_target_pairs={{0,4},{4,0},{8,12},{12,8},{16,20},{20,16},{24,28},{28,24},{1,2},{5... | collective-permute-start | bytes 552968 | tf_op jit(solution)/shard_map/ppermute | solution.py:619
